TPU v7x, 32 devices: a whole 2x2x4 slice. The times are simulated.
32 devices in a mesh: sec: 4 (over y, x), tile: 8 (over z, core).
Axes of the slice: x: 2, y: 2, z: 4, core: 2. Of those that a mesh axis runs over, the one named last changes fastest.
Arguments:
- beams: float32 [4, 2, 128, 2048], P('sec', None, 'tile'), may hold values from -6 to 6
- medium: float32 [4, 128, 2048], P('sec', 'tile'), may hold values from -0.3 to 0.3
Outputs:
- exit_fields: float32 [4, 2, 128, 2048], P('sec', None, 'tile')
All inputs are finite; a program needn't handle non-finite values.
Results may differ from a plain program's by a relative error of at most 0.00002.
Values sent between devices are 32-bit elements; how exact they have to be, the bound alone decides.
No kernel may reach another device: no remote copies, remote signals or barrier semaphores. Data moves between devices by JAX's collectives and lax.ppermute only.
A program may use at most 64 MiB of HBM per device.

v0:
```python
import jax
import jax.numpy as jnp
from jax import lax
from jax.sharding import PartitionSpec as P

HALO = 4


diffract_coef = 0.5
step_length = 0.65


def padded_2(block, sides, width):
    for axis, dim in sides:
        count = lax.axis_size(axis)
        forward = [(i, i + 1) for i in range(count - 1)]
        backward = [(target, source) for source, target in forward]
        low = lax.ppermute(
            lax.slice_in_dim(block, block.shape[dim] - width, None, axis=dim), axis, forward
        )
        high = lax.ppermute(lax.slice_in_dim(block, 0, width, axis=dim), axis, backward)
        block = jnp.concatenate([low, block, high], axis=dim)
    return block


def laplace(envelope):
    pads = [(0, 0)] * (envelope.ndim - 2) + [(1, 1), (1, 1)]
    padded = jnp.pad(envelope, pads)
    return (
        padded[..., :-2, 1:-1]
        + padded[..., 2:, 1:-1]
        + padded[..., 1:-1, :-2]
        + padded[..., 1:-1, 2:]
        - 4.0 * envelope
    )


def derivative(envelope, medium_ext, inside):
    masked = envelope * inside
    forcing = diffract_coef * laplace(masked) + medium_ext * masked
    return jnp.stack([-forcing[..., 1, :, :], forcing[..., 0, :, :]], axis=-3)


def advance(envelope, medium_ext, inside):
    half_length = 0.5 * step_length
    slope_one = derivative(envelope, medium_ext, inside)
    slope_two = derivative(envelope + half_length * slope_one, medium_ext, inside)
    slope_three = derivative(envelope + half_length * slope_two, medium_ext, inside)
    slope_four = derivative(envelope + step_length * slope_three, medium_ext, inside)
    return envelope + step_length / 6.0 * (
        slope_one + 2.0 * slope_two + 2.0 * slope_three + slope_four
    )


def per_device(beams, medium):
    tile_rows = medium.shape[1]
    rim_depth = HALO
    tile_count = lax.axis_size("tile")
    tile_place = lax.axis_index("tile")
    global_row = (
        lax.broadcasted_iota(jnp.int32, (tile_rows + 2 * rim_depth, 1), 0)
        + tile_place * tile_rows
        - rim_depth
    )
    inside = ((global_row >= 0) & (global_row < tile_rows * tile_count)).astype(jnp.float32)
    medium_ext = padded_2(medium, (("tile", 1),), rim_depth)
    every_slab = lax.all_gather(medium_ext, "sec", axis=0, tiled=True)

    def section(envelope, slab_piece):
        widened = padded_2(envelope, (("tile", 1),), rim_depth)
        widened = advance(widened, slab_piece, inside)
        result = widened[:, rim_depth : rim_depth + tile_rows, :]
        return (result, None)

    final_field, unused = lax.scan(section, beams[0], every_slab)
    return final_field[None]


def solution(mesh):
    placed = (P("sec", None, "tile", None), P("sec", "tile", None))
    return jax.shard_map(
        per_device,
        mesh=mesh,
        in_specs=placed,
        out_specs=P("sec", None, "tile", None),
        check_vma=False,
    )
```

profile of v0, /device:TPU:1, one launch (start us, length us, event | category | flops | bytes accessed | tf_op | source)
XLA Modules:
  0.0 60.5 jit_solution(7827189889581937877)
XLA Ops:
  0.0 0.9 %copy-done.2 = f32[1,16,2048]{2,1,0:T(8,128)S(1)} copy-done((f32[1,16,2048]{2,1,0:T(8,128)S(1)}, f32[1,16,2048]{2,1,0:T(8,128)}, u32[]{:S(2)}) %copy-start.2) | copy-done | bytes 131096
  0.9 4.6 %collective-permute-start.2 = (f32[1,4,2048]{2,1,0:T(4,128)S(1)}, f32[1,4,2048]{2,1,0:T(4,128)S(1)}, u32[]{:S(2)}, u32[]{:S(2)}) collective-permute-start(f32[1,4,2048]{2,1,0:T(4,128)S(1)} %get-tuple-element.90), channel_id=1, source_target_pairs={{0,1},{1,2},{2,3},{3,4},{4,5},{5,6},{6,7},{8,9},{9,10},{10,11},{11... | collective-permute-start | bytes 98312 | tf_op jit(solution)/shard_map/ppermute | solution.py:18
  5.5 1.9 %collective-permute-start.3 = (f32[1,4,2048]{2,1,0:T(4,128)S(1)}, f32[1,4,2048]{2,1,0:T(4,128)S(1)}, u32[]{:S(2)}, u32[]{:S(2)}) collective-permute-start(f32[1,4,2048]{2,1,0:T(4,128)S(1)} %get-tuple-element.91), channel_id=1, source_target_pairs={{1,0},{2,1},{3,2},{4,3},{5,4},{6,5},{7,6},{9,8},{10,9},{11,10},{12... | collective-permute-start | bytes 98312 | tf_op jit(solution)/shard_map/ppermute | solution.py:21
  7.5 3.3 %collective-permute-done.3 = f32[1,4,2048]{2,1,0:T(4,128)S(1)} collective-permute-done((f32[1,4,2048]{2,1,0:T(4,128)S(1)}, f32[1,4,2048]{2,1,0:T(4,128)S(1)}, u32[]{:S(2)}, u32[]{:S(2)}) %collective-permute-start.3) | collective-permute-done | bytes 32800 | tf_op jit(solution)/shard_map/ppermute | solution.py:21
  10.8 10.5 %all_gather.3 = f32[4,24,2048]{2,1,0:T(8,128)S(1)} all-gather(f32[1,24,2048]{2,1,0:T(8,128)S(1)} %pad_maximum_fusion.5), channel_id=1, replica_groups=mesh['sec'=4,'tile'=8] {'sec'}, dimensions={0}, use_global_device_ids=true | all-gather | bytes 983040 | tf_op jit(solution)/shard_map/all_gather | solution.py:67
  21.3 38.5 %while.13 = (s32[]{:T(128)}, f32[2,16,2048]{2,1,0:T(8,128)S(1)}, f32[4,24,2048]{2,1,0:T(8,128)S(1)}, s32[]{:T(128)}, s32[]{:T(128)}) while((s32[]{:T(128)}, f32[2,16,2048]{2,1,0:T(8,128)S(1)}, f32[4,24,2048]{2,1,0:T(8,128)S(1)}, s32[]{:T(128)}, s32[]{:T(128)}) %tuple.51), condition=%wide.region_1.2_spmd.clone, body=%wide.region_0.1_spmd.clone.sunk | while | flops 6127762 | bytes 15073917 | solution.py:75
  21.4 1.9 %collective-permute-start = (f32[2,4,2048]{2,1,0:T(4,128)S(1)}, f32[2,4,2048]{2,1,0:T(4,128)S(1)}, u32[]{:S(2)}, u32[]{:S(2)}) collective-permute-start(f32[2,4,2048]{2,1,0:T(4,128)S(1)} %get-tuple-element.129), channel_id=1, source_target_pairs={{1,0},{2,1},{3,2},{4,3},{5,4},{6,5},{7,6},{9,8},{10,9},{11,10},{12... | collective-permute-start | bytes 196616 | tf_op jit(solution)/shard_map/while/body/eval_jaxpr/ppermute | solution.py:21
  23.3 4.9 %collective-permute-start.1 = (f32[2,4,2048]{2,1,0:T(4,128)S(1)}, f32[2,4,2048]{2,1,0:T(4,128)S(1)}, u32[]{:S(2)}, u32[]{:S(2)}) collective-permute-start(f32[2,4,2048]{2,1,0:T(4,128)S(1)} %get-tuple-element.130), channel_id=1, source_target_pairs={{0,1},{1,2},{2,3},{3,4},{4,5},{5,6},{6,7},{8,9},{9,10},{10,11},{11... | collective-permute-start | bytes 196616 | tf_op jit(solution)/shard_map/while/body/eval_jaxpr/ppermute | solution.py:18
  28.3 1.3 %collective-permute-done.1 = f32[2,4,2048]{2,1,0:T(4,128)S(1)} collective-permute-done((f32[2,4,2048]{2,1,0:T(4,128)S(1)}, f32[2,4,2048]{2,1,0:T(4,128)S(1)}, u32[]{:S(2)}, u32[]{:S(2)}) %collective-permute-start.1) | collective-permute-done | bytes 65568 | tf_op jit(solution)/shard_map/while/body/eval_jaxpr/ppermute | solution.py:18
  29.6 0.3 fusion.62
  30.0 0.1 fusion.63
  30.1 0.3 fusion.64
  30.4 0.1 fusion.65
  30.5 0.3 fusion.66
  30.8 0.1 fusion.68
  31.0 0.3 fusion.69
  31.3 0.2 fusion.70
  31.5 1.9 %collective-permute-start = (f32[2,4,2048]{2,1,0:T(4,128)S(1)}, f32[2,4,2048]{2,1,0:T(4,128)S(1)}, u32[]{:S(2)}, u32[]{:S(2)}) collective-permute-start(f32[2,4,2048]{2,1,0:T(4,128)S(1)} %get-tuple-element.129), channel_id=1, source_target_pairs={{1,0},{2,1},{3,2},{4,3},{5,4},{6,5},{7,6},{9,8},{10,9},{11,10},{12... | collective-permute-start | bytes 196616 | tf_op jit(solution)/shard_map/while/body/eval_jaxpr/ppermute | solution.py:21
  33.4 4.3 %collective-permute-start.1 = (f32[2,4,2048]{2,1,0:T(4,128)S(1)}, f32[2,4,2048]{2,1,0:T(4,128)S(1)}, u32[]{:S(2)}, u32[]{:S(2)}) collective-permute-start(f32[2,4,2048]{2,1,0:T(4,128)S(1)} %get-tuple-element.130), channel_id=1, source_target_pairs={{0,1},{1,2},{2,3},{3,4},{4,5},{5,6},{6,7},{8,9},{9,10},{10,11},{11... | collective-permute-start | bytes 196616 | tf_op jit(solution)/shard_map/while/body/eval_jaxpr/ppermute | solution.py:18
  37.7 1.3 %collective-permute-done.1 = f32[2,4,2048]{2,1,0:T(4,128)S(1)} collective-permute-done((f32[2,4,2048]{2,1,0:T(4,128)S(1)}, f32[2,4,2048]{2,1,0:T(4,128)S(1)}, u32[]{:S(2)}, u32[]{:S(2)}) %collective-permute-start.1) | collective-permute-done | bytes 65568 | tf_op jit(solution)/shard_map/while/body/eval_jaxpr/ppermute | solution.py:18
  39.1 0.3 fusion.62
  39.4 0.1 fusion.63
  39.5 0.3 fusion.64
  39.9 0.1 fusion.65
  40.0 0.3 fusion.66
  40.3 0.1 fusion.68
  40.4 0.3 fusion.69
  40.7 0.2 fusion.70
  40.9 1.9 %collective-permute-start = (f32[2,4,2048]{2,1,0:T(4,128)S(1)}, f32[2,4,2048]{2,1,0:T(4,128)S(1)}, u32[]{:S(2)}, u32[]{:S(2)}) collective-permute-start(f32[2,4,2048]{2,1,0:T(4,128)S(1)} %get-tuple-element.129), channel_id=1, source_target_pairs={{1,0},{2,1},{3,2},{4,3},{5,4},{6,5},{7,6},{9,8},{10,9},{11,10},{12... | collective-permute-start | bytes 196616 | tf_op jit(solution)/shard_map/while/body/eval_jaxpr/ppermute | solution.py:21
  42.9 4.3 %collective-permute-start.1 = (f32[2,4,2048]{2,1,0:T(4,128)S(1)}, f32[2,4,2048]{2,1,0:T(4,128)S(1)}, u32[]{:S(2)}, u32[]{:S(2)}) collective-permute-start(f32[2,4,2048]{2,1,0:T(4,128)S(1)} %get-tuple-element.130), channel_id=1, source_target_pairs={{0,1},{1,2},{2,3},{3,4},{4,5},{5,6},{6,7},{8,9},{9,10},{10,11},{11... | collective-permute-start | bytes 196616 | tf_op jit(solution)/shard_map/while/body/eval_jaxpr/ppermute | solution.py:18
  47.2 1.3 %collective-permute-done.1 = f32[2,4,2048]{2,1,0:T(4,128)S(1)} collective-permute-done((f32[2,4,2048]{2,1,0:T(4,128)S(1)}, f32[2,4,2048]{2,1,0:T(4,128)S(1)}, u32[]{:S(2)}, u32[]{:S(2)}) %collective-permute-start.1) | collective-permute-done | bytes 65568 | tf_op jit(solution)/shard_map/while/body/eval_jaxpr/ppermute | solution.py:18
  48.6 0.3 fusion.62
  48.9 0.1 fusion.63
  49.0 0.3 fusion.64
  49.4 0.3 fusion.66
  49.8 0.1 fusion.68
  49.9 0.3 fusion.69
  50.2 0.2 fusion.70
  50.4 1.9 %collective-permute-start = (f32[2,4,2048]{2,1,0:T(4,128)S(1)}, f32[2,4,2048]{2,1,0:T(4,128)S(1)}, u32[]{:S(2)}, u32[]{:S(2)}) collective-permute-start(f32[2,4,2048]{2,1,0:T(4,128)S(1)} %get-tuple-element.129), channel_id=1, source_target_pairs={{1,0},{2,1},{3,2},{4,3},{5,4},{6,5},{7,6},{9,8},{10,9},{11,10},{12... | collective-permute-start | bytes 196616 | tf_op jit(solution)/shard_map/while/body/eval_jaxpr/ppermute | solution.py:21
  52.3 4.3 %collective-permute-start.1 = (f32[2,4,2048]{2,1,0:T(4,128)S(1)}, f32[2,4,2048]{2,1,0:T(4,128)S(1)}, u32[]{:S(2)}, u32[]{:S(2)}) collective-permute-start(f32[2,4,2048]{2,1,0:T(4,128)S(1)} %get-tuple-element.130), channel_id=1, source_target_pairs={{0,1},{1,2},{2,3},{3,4},{4,5},{5,6},{6,7},{8,9},{9,10},{10,11},{11... | collective-permute-start | bytes 196616 | tf_op jit(solution)/shard_map/while/body/eval_jaxpr/ppermute | solution.py:18
  56.7 1.3 %collective-permute-done.1 = f32[2,4,2048]{2,1,0:T(4,128)S(1)} collective-permute-done((f32[2,4,2048]{2,1,0:T(4,128)S(1)}, f32[2,4,2048]{2,1,0:T(4,128)S(1)}, u32[]{:S(2)}, u32[]{:S(2)}) %collective-permute-start.1) | collective-permute-done | bytes 65568 | tf_op jit(solution)/shard_map/while/body/eval_jaxpr/ppermute | solution.py:18
  58.0 0.3 fusion.62
  58.3 0.1 fusion.63
  58.5 0.3 fusion.64
  58.9 0.3 fusion.66
  59.3 0.3 fusion.69
  59.7 0.2 fusion.70
  59.8 0.7 %copy-done = f32[2,16,2048]{2,1,0:T(8,128)} copy-done((f32[2,16,2048]{2,1,0:T(8,128)}, f32[2,16,2048]{2,1,0:T(8,128)S(1)}, u32[]{:S(2)}) %copy-start) | copy-done | bytes 262168
  (46 shorter events, 1.5 us)
Async XLA Ops:
  0.0 0.9 %copy-start.2 = (f32[1,16,2048]{2,1,0:T(8,128)S(1)}, f32[1,16,2048]{2,1,0:T(8,128)}, u32[]{:S(2)}) copy-start(f32[1,16,2048]{2,1,0:T(8,128)} %param.5) | copy-start | bytes 393220
  0.9 6.5 %collective-permute-start.2 = (f32[1,4,2048]{2,1,0:T(4,128)S(1)}, f32[1,4,2048]{2,1,0:T(4,128)S(1)}, u32[]{:S(2)}, u32[]{:S(2)}) collective-permute-start(f32[1,4,2048]{2,1,0:T(4,128)S(1)} %get-tuple-element.90), channel_id=1, source_target_pairs={{0,1},{1,2},{2,3},{3,4},{4,5},{5,6},{6,7},{8,9},{9,10},{10,11},{11... | collective-permute-start | bytes 98312 | tf_op jit(solution)/shard_map/ppermute | solution.py:18
  5.5 5.2 %collective-permute-start.3 = (f32[1,4,2048]{2,1,0:T(4,128)S(1)}, f32[1,4,2048]{2,1,0:T(4,128)S(1)}, u32[]{:S(2)}, u32[]{:S(2)}) collective-permute-start(f32[1,4,2048]{2,1,0:T(4,128)S(1)} %get-tuple-element.91), channel_id=1, source_target_pairs={{1,0},{2,1},{3,2},{4,3},{5,4},{6,5},{7,6},{9,8},{10,9},{11,10},{12... | collective-permute-start | bytes 98312 | tf_op jit(solution)/shard_map/ppermute | solution.py:21
  10.8 10.6 %copy-start.1 = (f32[1,2,16,2048]{3,2,1,0:T(8,128)S(1)}, f32[1,2,16,2048]{3,2,1,0:T(8,128)}, u32[]{:S(2)}) copy-start(f32[1,2,16,2048]{3,2,1,0:T(8,128)} %param.4) | copy-start | bytes 786436
  21.4 6.9 %collective-permute-start = (f32[2,4,2048]{2,1,0:T(4,128)S(1)}, f32[2,4,2048]{2,1,0:T(4,128)S(1)}, u32[]{:S(2)}, u32[]{:S(2)}) collective-permute-start(f32[2,4,2048]{2,1,0:T(4,128)S(1)} %get-tuple-element.129), channel_id=1, source_target_pairs={{1,0},{2,1},{3,2},{4,3},{5,4},{6,5},{7,6},{9,8},{10,9},{11,10},{12... | collective-permute-start | bytes 196616 | tf_op jit(solution)/shard_map/while/body/eval_jaxpr/ppermute | solution.py:21
  23.3 6.2 %collective-permute-start.1 = (f32[2,4,2048]{2,1,0:T(4,128)S(1)}, f32[2,4,2048]{2,1,0:T(4,128)S(1)}, u32[]{:S(2)}, u32[]{:S(2)}) collective-permute-start(f32[2,4,2048]{2,1,0:T(4,128)S(1)} %get-tuple-element.130), channel_id=1, source_target_pairs={{0,1},{1,2},{2,3},{3,4},{4,5},{5,6},{6,7},{8,9},{9,10},{10,11},{11... | collective-permute-start | bytes 196616 | tf_op jit(solution)/shard_map/while/body/eval_jaxpr/ppermute | solution.py:18
  31.5 6.3 %collective-permute-start = (f32[2,4,2048]{2,1,0:T(4,128)S(1)}, f32[2,4,2048]{2,1,0:T(4,128)S(1)}, u32[]{:S(2)}, u32[]{:S(2)}) collective-permute-start(f32[2,4,2048]{2,1,0:T(4,128)S(1)} %get-tuple-element.129), channel_id=1, source_target_pairs={{1,0},{2,1},{3,2},{4,3},{5,4},{6,5},{7,6},{9,8},{10,9},{11,10},{12... | collective-permute-start | bytes 196616 | tf_op jit(solution)/shard_map/while/body/eval_jaxpr/ppermute | solution.py:21
  33.4 5.6 %collective-permute-start.1 = (f32[2,4,2048]{2,1,0:T(4,128)S(1)}, f32[2,4,2048]{2,1,0:T(4,128)S(1)}, u32[]{:S(2)}, u32[]{:S(2)}) collective-permute-start(f32[2,4,2048]{2,1,0:T(4,128)S(1)} %get-tuple-element.130), channel_id=1, source_target_pairs={{0,1},{1,2},{2,3},{3,4},{4,5},{5,6},{6,7},{8,9},{9,10},{10,11},{11... | collective-permute-start | bytes 196616 | tf_op jit(solution)/shard_map/while/body/eval_jaxpr/ppermute | solution.py:18
  40.9 6.3 %collective-permute-start = (f32[2,4,2048]{2,1,0:T(4,128)S(1)}, f32[2,4,2048]{2,1,0:T(4,128)S(1)}, u32[]{:S(2)}, u32[]{:S(2)}) collective-permute-start(f32[2,4,2048]{2,1,0:T(4,128)S(1)} %get-tuple-element.129), channel_id=1, source_target_pairs={{1,0},{2,1},{3,2},{4,3},{5,4},{6,5},{7,6},{9,8},{10,9},{11,10},{12... | collective-permute-start | bytes 196616 | tf_op jit(solution)/shard_map/while/body/eval_jaxpr/ppermute | solution.py:21
  42.9 5.6 %collective-permute-start.1 = (f32[2,4,2048]{2,1,0:T(4,128)S(1)}, f32[2,4,2048]{2,1,0:T(4,128)S(1)}, u32[]{:S(2)}, u32[]{:S(2)}) collective-permute-start(f32[2,4,2048]{2,1,0:T(4,128)S(1)} %get-tuple-element.130), channel_id=1, source_target_pairs={{0,1},{1,2},{2,3},{3,4},{4,5},{5,6},{6,7},{8,9},{9,10},{10,11},{11... | collective-permute-start | bytes 196616 | tf_op jit(solution)/shard_map/while/body/eval_jaxpr/ppermute | solution.py:18
  50.4 6.3 %collective-permute-start = (f32[2,4,2048]{2,1,0:T(4,128)S(1)}, f32[2,4,2048]{2,1,0:T(4,128)S(1)}, u32[]{:S(2)}, u32[]{:S(2)}) collective-permute-start(f32[2,4,2048]{2,1,0:T(4,128)S(1)} %get-tuple-element.129), channel_id=1, source_target_pairs={{1,0},{2,1},{3,2},{4,3},{5,4},{6,5},{7,6},{9,8},{10,9},{11,10},{12... | collective-permute-start | bytes 196616 | tf_op jit(solution)/shard_map/while/body/eval_jaxpr/ppermute | solution.py:21
  52.3 5.6 %collective-permute-start.1 = (f32[2,4,2048]{2,1,0:T(4,128)S(1)}, f32[2,4,2048]{2,1,0:T(4,128)S(1)}, u32[]{:S(2)}, u32[]{:S(2)}) collective-permute-start(f32[2,4,2048]{2,1,0:T(4,128)S(1)} %get-tuple-element.130), channel_id=1, source_target_pairs={{0,1},{1,2},{2,3},{3,4},{4,5},{5,6},{6,7},{8,9},{9,10},{10,11},{11... | collective-permute-start | bytes 196616 | tf_op jit(solution)/shard_map/while/body/eval_jaxpr/ppermute | solution.py:18
  59.8 0.7 %copy-start = (f32[2,16,2048]{2,1,0:T(8,128)}, f32[2,16,2048]{2,1,0:T(8,128)S(1)}, u32[]{:S(2)}) copy-start(f32[2,16,2048]{2,1,0:T(8,128)S(1)} %get-tuple-element.58) | copy-start | bytes 786436
where the time goes:
time: 60.9 us; the launch traced here: 60.5 us
  starting transfers between devices  31.9 us (52%)
  blocking collectives  10.5 us (17%)
  waiting for transfers between devices  8.32 us (14%)
  other arithmetic  7.34 us (12%)
  local copies, waits for them, and re-layouts  1.8 us (3%)
    ppermute x5, starting transfers between devices, padded_2(): lax.ppermute(lax.slice_in_dim(block, block.shape[dim] - width, None, axis...  22.3 us
    all_gather x1, blocking collectives, per_device(): every_slab = lax.all_gather(medium_ext, 'sec', axis=0, tiled=True)  10.5 us
    ppermute x5, starting transfers between devices, padded_2(): lax.ppermute(lax.slice_in_dim(block, 0, width, axis=dim), axis, backward)  9.6 us
    ppermute x5, waiting for transfers between devices, padded_2(): lax.ppermute(lax.slice_in_dim(block, block.shape[dim] - width, None, axis...  5.02 us
    add x16, other arithmetic, derivative(): forcing = diffract_coef * laplace(masked) + medium_ext * masked  4.4 us
    ppermute x5, waiting for transfers between devices, padded_2(): lax.ppermute(lax.slice_in_dim(block, 0, width, axis=dim), axis, backward)  3.3 us
    mul x20, other arithmetic, derivative(): masked = envelope * inside  1.79 us
    unnamed x6, local copies, waits for them, and re-layouts  1.61 us
  transfers between devices with their start and end apart: 10, of which 5 were waited for; matrix products, arithmetic and copies ran while one was open for 0% of the time, Pallas kernels for 0%

commit v1 on v0

v1 whole, which is shorter than its diff:
```python
import functools

import jax
import jax.numpy as jnp
from jax import lax
from jax.experimental import pallas as pl
from jax.experimental.pallas import tpu as pltpu
from jax.sharding import PartitionSpec as P

AXES = ("sec", "tile")
LANES = 128
SUBLANES = 8
STAGES = 4

diffract_coef = 0.5
step_length = 0.65


def sec_swap(sec, tiles, k):
    return [(s * tiles + t, (s ^ k) * tiles + t) for s in range(sec) for t in range(tiles)]


def pair_swap(sec, tiles):
    return [(s * tiles + t, s * tiles + (t ^ 1)) for s in range(sec) for t in range(tiles)]


def rim_swap(sec, tiles):
    out = []
    for s in range(sec):
        for t in range(tiles):
            if 0 < t < tiles - 1:
                out.append((s * tiles + t, s * tiles + ((t + 1) ^ 1) - 1))
            else:
                out.append((s * tiles + t, (s ^ 1) * tiles + t))
    return out


def field_kernel(place_ref, *refs, sections, first, rows, cols, steps):
    own_b, pair_b, rim_b = refs[:3]
    own_m = refs[3 : 3 + sections]
    pair_m = refs[3 + sections : 3 + 2 * sections]
    rim_m = refs[3 + 2 * sections : 3 + 3 * sections]
    out_ref = refs[3 + 3 * sections]
    field_a, field_b, work_a, work_b, med, coef = refs[4 + 3 * sections :]
    sec, odd, edge = place_ref[0], place_ref[1], place_ref[2]
    chunks = cols // LANES
    pad = SUBLANES
    depth = STAGES * steps
    mid = pad + rows
    pair_at = pl.multiple_of(jnp.where(odd == 1, pad, mid + rows), SUBLANES)
    rim_at = pl.multiple_of(jnp.where(odd == 1, mid + rows, pad), SUBLANES)
    is_edge = edge == 1

    high = 2 * mid + rows
    row = lax.broadcasted_iota(jnp.int32, (high, LANES), 0)
    outside = is_edge & (row >= rim_at) & (row < rim_at + rows)
    for stage in range(STAGES):
        scale = diffract_coef * step_length / (STAGES - stage)
        coef[stage] = jnp.where(outside, 0.0, scale)

    def load(j, carry):
        col = pl.ds(pl.multiple_of(j * LANES, LANES), LANES)
        for t in range(0, rows, SUBLANES):
            src = pl.ds(t, SUBLANES)
            for part in range(2):
                field_a[j, part, pl.ds(mid + t, SUBLANES), :] = own_b[part, src, col]
                field_a[j, part, pl.ds(pair_at + t, SUBLANES), :] = pair_b[part, src, col]
                field_a[j, part, pl.ds(rim_at + t, SUBLANES), :] = jnp.where(
                    is_edge, 0.0, rim_b[part, src, col]
                )
            for k in range(sections):
                slot = sec ^ k
                for at, piece in ((mid, own_m), (pair_at, pair_m), (rim_at, rim_m)):
                    value = piece[k][0, src, col] * (1.0 / diffract_coef) - 4.0
                    med[slot, j, pl.ds(at + t, SUBLANES), :] = value
        return carry

    lax.fori_loop(0, chunks, load, 0)

    lane = lax.broadcasted_iota(jnp.int32, (SUBLANES, LANES), 1)
    low_lane, high_lane = lane == 0, lane == LANES - 1
    begin, end = field_a, field_b
    level = 0
    for step in range(steps):
        source = begin
        for stage in range(STAGES):
            level += 1
            reach = depth - level
            start = mid - reach
            blocks = -(-(rows + 2 * reach) // SUBLANES)
            target = (work_a, work_b, work_a, end)[stage]
            last = level == depth
            for j in range(chunks):
                for block in range(blocks):
                    at = start + SUBLANES * block
                    here = pl.ds(at, SUBLANES)
                    m = med[first + step, j, here, :]
                    g = coef[stage, here, :]
                    drive = []
                    for part in range(2):
                        w = source[j, part, here, :]
                        rows_sum = (
                            source[j, part, pl.ds(at - 1, SUBLANES), :]
                            + source[j, part, pl.ds(at + 1, SUBLANES), :]
                        )
                        before = source[j - 1, part, here, :] if j > 0 else jnp.zeros_like(w)
                        after = source[j + 1, part, here, :] if j + 1 < chunks else jnp.zeros_like(w)
                        left = pltpu.roll(jnp.where(high_lane, before, w), 1, 1)
                        right = pltpu.roll(jnp.where(low_lane, after, w), LANES - 1, 1)
                        drive.append(g * (rows_sum + (left + right) + m * w))
                    re = begin[j, 0, here, :] - drive[1]
                    im = begin[j, 1, here, :] + drive[0]
                    if last:
                        spot = (pl.ds(SUBLANES * block, SUBLANES), pl.ds(j * LANES, LANES))
                        out_ref[0, spot[0], spot[1]] = re
                        out_ref[1, spot[0], spot[1]] = im
                    else:
                        target[j, 0, here, :] = re
                        target[j, 1, here, :] = im
            source = target
        begin, end = end, begin


def per_device(beams, medium):
    sections, tiles = lax.axis_size("sec"), lax.axis_size("tile")
    _, rows, cols = medium.shape
    sec, tile = lax.axis_index("sec"), lax.axis_index("tile")
    place = jnp.stack(
        [sec, tile % 2, ((tile == 0) | (tile == tiles - 1)).astype(jnp.int32)]
    ).astype(jnp.int32)
    swap = lambda value, pairs: lax.ppermute(value, AXES, pairs)
    pair, rim = pair_swap(sections, tiles), rim_swap(sections, tiles)

    own = [medium] + [
        swap(medium, sec_swap(sections, tiles, k)) for k in range(1, sections)
    ]
    pair_field, rim_field = swap(beams, pair), swap(beams, rim)
    own[1:] = lax.optimization_barrier(tuple(own[1:]) + (rim_field,))[:-1]
    pair_pieces = [swap(piece, pair) for piece in own]
    rim_pieces = [swap(piece, rim) for piece in own]

    chunks = cols // LANES
    high = 2 * SUBLANES + 3 * rows
    field = beams
    group = rows // STAGES
    for first in range(0, sections, group):
        steps = min(group, sections - first)
        if first > 0:
            pair_field, rim_field = swap(field, pair), swap(field, rim)
        whole = pl.BlockSpec(memory_space=pltpu.VMEM)
        field = pl.pallas_call(
            functools.partial(
                field_kernel, sections=sections, first=first, rows=rows, cols=cols, steps=steps
            ),
            out_shape=jax.ShapeDtypeStruct((2, rows, cols), jnp.float32),
            in_specs=[pl.BlockSpec(memory_space=pltpu.SMEM)] + [whole] * (3 + 3 * sections),
            out_specs=whole,
            scratch_shapes=[pltpu.VMEM((chunks, 2, high, LANES), jnp.float32)] * 4
            + [
                pltpu.VMEM((sections, chunks, high, LANES), jnp.float32),
                pltpu.VMEM((STAGES, high, LANES), jnp.float32),
            ],
            compiler_params=pltpu.CompilerParams(vmem_limit_bytes=48 * 2**20),
            name="sections_of_field",
        )(place, field.reshape(2, rows, cols), pair_field.reshape(2, rows, cols),
          rim_field.reshape(2, rows, cols), *own, *pair_pieces, *rim_pieces)[None]
    return field


def solution(mesh):
    placed = (P("sec", None, "tile", None), P("sec", "tile", None))
    return jax.shard_map(
        per_device,
        mesh=mesh,
        in_specs=placed,
        out_specs=P("sec", None, "tile", None),
        check_vma=False,
    )
```

time: 60.9 us -> 32.1 us (0.53)
  the two profiles are of different devices: /device:TPU:1 before, /device:TPU:0 now
where the time goes in v1:
time: 32.1 us; the launch traced here: 31.9 us
  starting transfers between devices  11.9 us (37%)
  waiting for transfers between devices  11.6 us (36%)
  Pallas kernels  6.45 us (20%)
  local copies, waits for them, and re-layouts  1.85 us (6%)
    ppermute x13, starting transfers between devices, per_device(): swap = lambda value, pairs: lax.ppermute(value, AXES, pairs)  11.9 us
    ppermute x13, waiting for transfers between devices, per_device(): swap = lambda value, pairs: lax.ppermute(value, AXES, pairs)  11.6 us
    pallas_call x1, Pallas kernels, per_device(): pl.pallas_call(functools.partial(field_kernel, sections=sections, first=f...  6.45 us
    unnamed x4, local copies, waits for them, and re-layouts  1.85 us
  transfers between devices with their start and end apart: 13, of which 4 were waited for; matrix products, arithmetic and copies ran while one was open for 0% of the time, Pallas kernels for 0%

profile of v1, /device:TPU:0, one launch (start us, length us, event | category | flops | bytes accessed | tf_op | source)
XLA Modules:
  0.0 31.9 jit_solution(7297187561112818858)
XLA Ops:
  0.0 2.9 %collective-permute-start.1 = (f32[1,2,16,2048]{3,2,1,0:T(8,128)}, f32[1,2,16,2048]{3,2,1,0:T(8,128)S(1)}, u32[]{:S(2)}, u32[]{:S(2)}) collective-permute-start(f32[1,2,16,2048]{3,2,1,0:T(8,128)} %param.2), channel_id=1, source_target_pairs={{0,8},{1,2},{2,1},{3,4},{4,3},{5,6},{6,5},{7,15},{8,0},{9,10},{10,... | collective-permute-start | bytes 786440 | tf_op jit(solution)/shard_map/ppermute | solution.py:131
  2.9 1.5 %collective-permute-start.4 = (f32[1,16,2048]{2,1,0:T(8,128)}, f32[1,16,2048]{2,1,0:T(8,128)S(1)}, u32[]{:S(2)}, u32[]{:S(2)}) collective-permute-start(f32[1,16,2048]{2,1,0:T(8,128)} %refs_3_.1), channel_id=1, source_target_pairs={{0,24},{1,25},{2,26},{3,27},{4,28},{5,29},{6,30},{7,31},{8,16},{9,... | collective-permute-start | bytes 393224 | tf_op jit(solution)/shard_map/ppermute | solution.py:131
  4.4 0.0 collective-permute-start.3
  4.5 2.0 %collective-permute-start.2 = (f32[1,16,2048]{2,1,0:T(8,128)}, f32[1,16,2048]{2,1,0:T(8,128)S(1)}, u32[]{:S(2)}, u32[]{:S(2)}) collective-permute-start(f32[1,16,2048]{2,1,0:T(8,128)} %refs_3_.1), channel_id=1, source_target_pairs={{0,8},{1,9},{2,10},{3,11},{4,12},{5,13},{6,14},{7,15},{8,0},{9,1},... | collective-permute-start | bytes 393224 | tf_op jit(solution)/shard_map/ppermute | solution.py:131
  6.4 0.0 collective-permute-start
  6.4 6.8 %collective-permute-done.4.refs_6_ = f32[1,16,2048]{2,1,0:T(8,128)S(1)} collective-permute-done((f32[1,16,2048]{2,1,0:T(8,128)}, f32[1,16,2048]{2,1,0:T(8,128)S(1)}, u32[]{:S(2)}, u32[]{:S(2)}) %collective-permute-start.4) | collective-permute-done | bytes 131104 | tf_op jit(solution)/shard_map/ppermute | solution.py:131
  13.2 0.0 collective-permute-start.5
  13.2 0.0 collective-permute-done.3.refs_5_
  13.2 1.5 %collective-permute-start.9 = (f32[1,16,2048]{2,1,0:T(8,128)}, f32[1,16,2048]{2,1,0:T(8,128)S(1)}, u32[]{:S(2)}, u32[]{:S(2)}) collective-permute-start(f32[1,16,2048]{2,1,0:T(8,128)} %refs_3_.1), channel_id=1, source_target_pairs={{0,8},{1,2},{2,1},{3,4},{4,3},{5,6},{6,5},{7,15},{8,0},{9,10},{10,... | collective-permute-start | bytes 393224 | tf_op jit(solution)/shard_map/ppermute | solution.py:131
  14.7 0.0 collective-permute-done.2.refs_4_
  14.7 0.0 collective-permute-done.1
  14.7 0.5 %collective-permute-start.10 = (f32[1,16,2048]{2,1,0:T(8,128)S(1)}, f32[1,16,2048]{2,1,0:T(8,128)S(1)}, u32[]{:S(2)}, u32[]{:S(2)}) collective-permute-start(f32[1,16,2048]{2,1,0:T(8,128)S(1)} %collective-permute-done.2.refs_4_), channel_id=1, source_target_pairs={{0,8},{1,2},{2,1},{3,4},{4,3},{5,6},{6,5},{7,15},{8,0},{9,10},{10,... | collective-permute-start | bytes 393224 | tf_op jit(solution)/shard_map/ppermute | solution.py:131
  15.2 0.2 collective-permute-start.6
  15.5 0.0 collective-permute-done.5.refs_7_
  15.5 1.5 %collective-permute-start.11 = (f32[1,16,2048]{2,1,0:T(8,128)S(1)}, f32[1,16,2048]{2,1,0:T(8,128)S(1)}, u32[]{:S(2)}, u32[]{:S(2)}) collective-permute-start(f32[1,16,2048]{2,1,0:T(8,128)S(1)} %collective-permute-done.3.refs_5_), channel_id=1, source_target_pairs={{0,8},{1,2},{2,1},{3,4},{4,3},{5,6},{6,5},{7,15},{8,0},{9,10},{10,... | collective-permute-start | bytes 393224 | tf_op jit(solution)/shard_map/ppermute | solution.py:131
  17.0 1.4 %collective-permute-done.9.refs_11_ = f32[1,16,2048]{2,1,0:T(8,128)S(1)} collective-permute-done((f32[1,16,2048]{2,1,0:T(8,128)}, f32[1,16,2048]{2,1,0:T(8,128)S(1)}, u32[]{:S(2)}, u32[]{:S(2)}) %collective-permute-start.9) | collective-permute-done | bytes 131104 | tf_op jit(solution)/shard_map/ppermute | solution.py:131
  18.4 0.2 collective-permute-start.7
  18.6 0.0 collective-permute-done
  18.6 1.5 %collective-permute-start.12 = (f32[1,16,2048]{2,1,0:T(8,128)S(1)}, f32[1,16,2048]{2,1,0:T(8,128)S(1)}, u32[]{:S(2)}, u32[]{:S(2)}) collective-permute-start(f32[1,16,2048]{2,1,0:T(8,128)S(1)} %collective-permute-done.4.refs_6_), channel_id=1, source_target_pairs={{0,8},{1,2},{2,1},{3,4},{4,3},{5,6},{6,5},{7,15},{8,0},{9,10},{10,... | collective-permute-start | bytes 393224 | tf_op jit(solution)/shard_map/ppermute | solution.py:131
  20.1 0.0 collective-permute-done.10.refs_12_
  20.1 0.0 collective-permute-start.8
  20.1 0.1 pad_add_fusion.place_ref
  20.2 0.0 collective-permute-done.6.refs_8_
  20.2 1.0 %collective-permute-done.11.refs_13_ = f32[1,16,2048]{2,1,0:T(8,128)S(1)} collective-permute-done((f32[1,16,2048]{2,1,0:T(8,128)S(1)}, f32[1,16,2048]{2,1,0:T(8,128)S(1)}, u32[]{:S(2)}, u32[]{:S(2)}) %collective-permute-start.11) | collective-permute-done | bytes 131104 | tf_op jit(solution)/shard_map/ppermute | solution.py:131
  21.2 0.0 collective-permute-done.7.refs_9_
  21.2 2.4 %collective-permute-done.12.refs_14_ = f32[1,16,2048]{2,1,0:T(8,128)S(1)} collective-permute-done((f32[1,16,2048]{2,1,0:T(8,128)S(1)}, f32[1,16,2048]{2,1,0:T(8,128)S(1)}, u32[]{:S(2)}, u32[]{:S(2)}) %collective-permute-start.12) | collective-permute-done | bytes 131104 | tf_op jit(solution)/shard_map/ppermute | solution.py:131
  23.6 0.0 collective-permute-done.8.refs_10_
  23.6 0.0 copy-start
  23.6 0.9 %copy-done = f32[1,2,16,2048]{3,2,1,0:T(8,128)S(1)} copy-done((f32[1,2,16,2048]{3,2,1,0:T(8,128)S(1)}, f32[1,2,16,2048]{3,2,1,0:T(8,128)}, u32[]{:S(2)}) %copy-start) | copy-done | bytes 262168
  24.5 0.0 copy-start.1
  24.5 0.9 %copy-done.1 = f32[1,16,2048]{2,1,0:T(8,128)S(1)} copy-done((f32[1,16,2048]{2,1,0:T(8,128)S(1)}, f32[1,16,2048]{2,1,0:T(8,128)}, u32[]{:S(2)}) %copy-start.1) | copy-done | bytes 131096
  25.4 6.5 %sections_of_field.1 = f32[2,16,2048]{2,1,0:T(8,128)} custom-call(s32[3]{0:T(128)S(1)} %pad_add_fusion.place_ref, f32[2,16,2048]{2,1,0:T(8,128)S(1)} %bitcast.7, f32[2,16,2048]{2,1,0:T(8,128)S(1)} %bitcast.9, f32[2,16,2048]{2,1,0:T(8,128)S(1)} %bitcast.8, f32[1,16,2048]{2,1,0:T(8,128)S(1)} %copy-done.1, f32[1,16,2048]{2,1,0:T(8,128)S(1)} %collective-permute-done.2.refs_4_, ...), custom_call_target="tpu_custom_call" | custom-call | tf_op jit(solution)/shard_map/sections_of_field/pallas_call | solution.py:151
Async XLA Ops:
  0.0 14.7 %collective-permute-start.1 = (f32[1,2,16,2048]{3,2,1,0:T(8,128)}, f32[1,2,16,2048]{3,2,1,0:T(8,128)S(1)}, u32[]{:S(2)}, u32[]{:S(2)}) collective-permute-start(f32[1,2,16,2048]{3,2,1,0:T(8,128)} %param.2), channel_id=1, source_target_pairs={{0,8},{1,2},{2,1},{3,4},{4,3},{5,6},{6,5},{7,15},{8,0},{9,10},{10,... | collective-permute-start | bytes 786440 | tf_op jit(solution)/shard_map/ppermute | solution.py:131
  2.9 10.3 %collective-permute-start.4 = (f32[1,16,2048]{2,1,0:T(8,128)}, f32[1,16,2048]{2,1,0:T(8,128)S(1)}, u32[]{:S(2)}, u32[]{:S(2)}) collective-permute-start(f32[1,16,2048]{2,1,0:T(8,128)} %refs_3_.1), channel_id=1, source_target_pairs={{0,24},{1,25},{2,26},{3,27},{4,28},{5,29},{6,30},{7,31},{8,16},{9,... | collective-permute-start | bytes 393224 | tf_op jit(solution)/shard_map/ppermute | solution.py:131
  4.4 8.8 %collective-permute-start.3 = (f32[1,16,2048]{2,1,0:T(8,128)}, f32[1,16,2048]{2,1,0:T(8,128)S(1)}, u32[]{:S(2)}, u32[]{:S(2)}) collective-permute-start(f32[1,16,2048]{2,1,0:T(8,128)} %refs_3_.1), channel_id=1, source_target_pairs={{0,16},{1,17},{2,18},{3,19},{4,20},{5,21},{6,22},{7,23},{8,24},{9,... | collective-permute-start | bytes 393224 | tf_op jit(solution)/shard_map/ppermute | solution.py:131
  4.5 10.2 %collective-permute-start.2 = (f32[1,16,2048]{2,1,0:T(8,128)}, f32[1,16,2048]{2,1,0:T(8,128)S(1)}, u32[]{:S(2)}, u32[]{:S(2)}) collective-permute-start(f32[1,16,2048]{2,1,0:T(8,128)} %refs_3_.1), channel_id=1, source_target_pairs={{0,8},{1,9},{2,10},{3,11},{4,12},{5,13},{6,14},{7,15},{8,0},{9,1},... | collective-permute-start | bytes 393224 | tf_op jit(solution)/shard_map/ppermute | solution.py:131
  6.4 12.2 %collective-permute-start = (f32[1,2,16,2048]{3,2,1,0:T(8,128)}, f32[1,2,16,2048]{3,2,1,0:T(8,128)S(1)}, u32[]{:S(2)}, u32[]{:S(2)}) collective-permute-start(f32[1,2,16,2048]{3,2,1,0:T(8,128)} %param.2), channel_id=1, source_target_pairs={{0,1},{1,0},{2,3},{3,2},{4,5},{5,4},{6,7},{7,6},{8,9},{9,8},{10,11... | collective-permute-start | bytes 786440 | tf_op jit(solution)/shard_map/ppermute | solution.py:131
  13.2 2.3 %collective-permute-start.5 = (f32[1,16,2048]{2,1,0:T(8,128)}, f32[1,16,2048]{2,1,0:T(8,128)S(1)}, u32[]{:S(2)}, u32[]{:S(2)}) collective-permute-start(f32[1,16,2048]{2,1,0:T(8,128)} %refs_3_.1), channel_id=1, source_target_pairs={{0,1},{1,0},{2,3},{3,2},{4,5},{5,4},{6,7},{7,6},{8,9},{9,8},{10,11... | collective-permute-start | bytes 393224 | tf_op jit(solution)/shard_map/ppermute | solution.py:131
  13.2 5.2 %collective-permute-start.9 = (f32[1,16,2048]{2,1,0:T(8,128)}, f32[1,16,2048]{2,1,0:T(8,128)S(1)}, u32[]{:S(2)}, u32[]{:S(2)}) collective-permute-start(f32[1,16,2048]{2,1,0:T(8,128)} %refs_3_.1), channel_id=1, source_target_pairs={{0,8},{1,2},{2,1},{3,4},{4,3},{5,6},{6,5},{7,15},{8,0},{9,10},{10,... | collective-permute-start | bytes 393224 | tf_op jit(solution)/shard_map/ppermute | solution.py:131
  14.7 5.4 %collective-permute-start.10 = (f32[1,16,2048]{2,1,0:T(8,128)S(1)}, f32[1,16,2048]{2,1,0:T(8,128)S(1)}, u32[]{:S(2)}, u32[]{:S(2)}) collective-permute-start(f32[1,16,2048]{2,1,0:T(8,128)S(1)} %collective-permute-done.2.refs_4_), channel_id=1, source_target_pairs={{0,8},{1,2},{2,1},{3,4},{4,3},{5,6},{6,5},{7,15},{8,0},{9,10},{10,... | collective-permute-start | bytes 393224 | tf_op jit(solution)/shard_map/ppermute | solution.py:131
  15.2 5.0 %collective-permute-start.6 = (f32[1,16,2048]{2,1,0:T(8,128)S(1)}, f32[1,16,2048]{2,1,0:T(8,128)S(1)}, u32[]{:S(2)}, u32[]{:S(2)}) collective-permute-start(f32[1,16,2048]{2,1,0:T(8,128)S(1)} %collective-permute-done.2.refs_4_), channel_id=1, source_target_pairs={{0,1},{1,0},{2,3},{3,2},{4,5},{5,4},{6,7},{7,6},{8,9},{9,8},{10,11... | collective-permute-start | bytes 393224 | tf_op jit(solution)/shard_map/ppermute | solution.py:131
  15.5 5.7 %collective-permute-start.11 = (f32[1,16,2048]{2,1,0:T(8,128)S(1)}, f32[1,16,2048]{2,1,0:T(8,128)S(1)}, u32[]{:S(2)}, u32[]{:S(2)}) collective-permute-start(f32[1,16,2048]{2,1,0:T(8,128)S(1)} %collective-permute-done.3.refs_5_), channel_id=1, source_target_pairs={{0,8},{1,2},{2,1},{3,4},{4,3},{5,6},{6,5},{7,15},{8,0},{9,10},{10,... | collective-permute-start | bytes 393224 | tf_op jit(solution)/shard_map/ppermute | solution.py:131
  18.4 2.8 %collective-permute-start.7 = (f32[1,16,2048]{2,1,0:T(8,128)S(1)}, f32[1,16,2048]{2,1,0:T(8,128)S(1)}, u32[]{:S(2)}, u32[]{:S(2)}) collective-permute-start(f32[1,16,2048]{2,1,0:T(8,128)S(1)} %collective-permute-done.3.refs_5_), channel_id=1, source_target_pairs={{0,1},{1,0},{2,3},{3,2},{4,5},{5,4},{6,7},{7,6},{8,9},{9,8},{10,11... | collective-permute-start | bytes 393224 | tf_op jit(solution)/shard_map/ppermute | solution.py:131
  18.6 5.0 %collective-permute-start.12 = (f32[1,16,2048]{2,1,0:T(8,128)S(1)}, f32[1,16,2048]{2,1,0:T(8,128)S(1)}, u32[]{:S(2)}, u32[]{:S(2)}) collective-permute-start(f32[1,16,2048]{2,1,0:T(8,128)S(1)} %collective-permute-done.4.refs_6_), channel_id=1, source_target_pairs={{0,8},{1,2},{2,1},{3,4},{4,3},{5,6},{6,5},{7,15},{8,0},{9,10},{10,... | collective-permute-start | bytes 393224 | tf_op jit(solution)/shard_map/ppermute | solution.py:131
  20.1 3.5 %collective-permute-start.8 = (f32[1,16,2048]{2,1,0:T(8,128)S(1)}, f32[1,16,2048]{2,1,0:T(8,128)S(1)}, u32[]{:S(2)}, u32[]{:S(2)}) collective-permute-start(f32[1,16,2048]{2,1,0:T(8,128)S(1)} %collective-permute-done.4.refs_6_), channel_id=1, source_target_pairs={{0,1},{1,0},{2,3},{3,2},{4,5},{5,4},{6,7},{7,6},{8,9},{9,8},{10,11... | collective-permute-start | bytes 393224 | tf_op jit(solution)/shard_map/ppermute | solution.py:131
  23.6 1.0 %copy-start = (f32[1,2,16,2048]{3,2,1,0:T(8,128)S(1)}, f32[1,2,16,2048]{3,2,1,0:T(8,128)}, u32[]{:S(2)}) copy-start(f32[1,2,16,2048]{3,2,1,0:T(8,128)} %param.2) | copy-start | bytes 786436
  24.5 0.9 %copy-start.1 = (f32[1,16,2048]{2,1,0:T(8,128)S(1)}, f32[1,16,2048]{2,1,0:T(8,128)}, u32[]{:S(2)}) copy-start(f32[1,16,2048]{2,1,0:T(8,128)} %refs_3_.1) | copy-start | bytes 393220

commit v2 on v1

v2 whole, which is shorter than its diff:
```python
import functools

import jax
import jax.numpy as jnp
from jax import lax
from jax.experimental import pallas as pl
from jax.experimental.pallas import tpu as pltpu
from jax.sharding import PartitionSpec as P

AXES = ("sec", "tile")
LANES = 128
SUBLANES = 8
STAGES = 4

diffract_coef = 0.5
step_length = 0.65


def sec_swap(sec, tiles, k):
    return [(s * tiles + t, (s ^ k) * tiles + t) for s in range(sec) for t in range(tiles)]


def pair_swap(sec, tiles):
    return [(s * tiles + t, s * tiles + (t ^ 1)) for s in range(sec) for t in range(tiles)]


def rim_swap(sec, tiles):
    out = []
    for s in range(sec):
        for t in range(tiles):
            if 0 < t < tiles - 1:
                out.append((s * tiles + t, s * tiles + ((t + 1) ^ 1) - 1))
            else:
                out.append((s * tiles + t, (s ^ 1) * tiles + t))
    return out


def stage_scale(stage):
    return diffract_coef * step_length / (STAGES - stage)


def run_stage(source, begin, med, start, blocks, chunks, scale_of, store):
    lane = lax.broadcasted_iota(jnp.int32, (SUBLANES, LANES), 1)
    low_lane, high_lane = lane == 0, lane == LANES - 1
    for j in range(chunks):
        for block in range(blocks):
            at = start + SUBLANES * block
            here = pl.ds(at, SUBLANES)
            m = med[j, here, :]
            g = scale_of(here)
            drive = []
            for part in range(2):
                w = source[j, part, here, :]
                rows_sum = (
                    source[j, part, pl.ds(at - 1, SUBLANES), :]
                    + source[j, part, pl.ds(at + 1, SUBLANES), :]
                )
                before = source[j - 1, part, here, :] if j > 0 else jnp.zeros_like(w)
                after = source[j + 1, part, here, :] if j + 1 < chunks else jnp.zeros_like(w)
                left = pltpu.roll(jnp.where(high_lane, before, w), 1, 1)
                right = pltpu.roll(jnp.where(low_lane, after, w), LANES - 1, 1)
                drive.append(g * (rows_sum + (left + right) + m * w))
            store(j, block, 0, here, begin[j, 0, here, :] - drive[1])
            store(j, block, 1, here, begin[j, 1, here, :] + drive[0])


def row_groups(rows):
    return range(0, rows, SUBLANES)


def columns(j):
    return pl.ds(pl.multiple_of(j * LANES, LANES), LANES)


def to_medium_term(value):
    return value * (1.0 / diffract_coef) - 4.0


def inner_kernel(place_ref, *refs, sections, first, rows, cols, steps):
    own_b, pair_b, rim_b = refs[:3]
    own_m = refs[3 : 3 + sections]
    pair_m = refs[3 + sections]
    edge_ref = refs[4 + sections]
    field_a, field_b, work_a, work_b, med = refs[5 + sections :]
    sec, odd, edge = place_ref[0], place_ref[1], place_ref[2]
    chunks = cols // LANES
    depth = STAGES * steps
    mid = SUBLANES + rows
    pair_at = pl.multiple_of(jnp.where(odd == 1, SUBLANES, mid + rows), SUBLANES)
    rim_at = pl.multiple_of(jnp.where(odd == 1, mid + rows, SUBLANES), SUBLANES)
    is_edge = edge == 1

    def load(j, carry):
        col = columns(j)
        for t in row_groups(rows):
            src = pl.ds(t, SUBLANES)
            for part in range(2):
                field_a[j, part, pl.ds(mid + t, SUBLANES), :] = own_b[part, src, col]
                field_a[j, part, pl.ds(pair_at + t, SUBLANES), :] = pair_b[part, src, col]
                field_a[j, part, pl.ds(rim_at + t, SUBLANES), :] = jnp.where(
                    is_edge, 0.0, rim_b[part, src, col]
                )
            for k in range(sections):
                slot = sec ^ k
                med[slot, j, pl.ds(mid + t, SUBLANES), :] = to_medium_term(own_m[k][0, src, col])
                med[slot, j, pl.ds(pair_at + t, SUBLANES), :] = to_medium_term(
                    pair_m[k, src, col]
                )
        return carry

    lax.fori_loop(0, chunks, load, 0)

    low = pl.multiple_of(jnp.where(odd == 1, SUBLANES, mid), SUBLANES)
    begin, end = field_a, field_b
    level = 0
    for step in range(steps):
        source = begin
        for stage in range(STAGES):
            level += 1
            if level == depth:
                break
            target = (work_a, work_b, work_a, end)[stage]

            def store(j, block, part, here, value, target=target):
                target[j, part, here, :] = value

            run_stage(
                source, begin, med.at[first + step], low + level,
                -(-(2 * (rows - level)) // SUBLANES), chunks,
                lambda here, stage=stage: stage_scale(stage), store,
            )
            edge_at = jnp.where(odd == 1, mid + rows - SUBLANES - level, mid + level)
            for j in range(chunks):
                for part in range(2):
                    edge_ref[level - 1, j, part, :, :] = target[
                        j, part, pl.ds(edge_at, SUBLANES), :
                    ]
            source = target
        begin, end = end, begin


def outer_kernel(place_ref, *refs, sections, first, rows, cols, steps):
    own_b, rim_b = refs[:2]
    own_m = refs[2 : 2 + sections]
    rim_m, edge_ref, out_ref = refs[2 + sections : 5 + sections]
    field_a, field_b, work_a, work_b, med, coef = refs[5 + sections :]
    sec, odd, edge = place_ref[0], place_ref[1], place_ref[2]
    chunks = cols // LANES
    depth = STAGES * steps
    mid = SUBLANES + rows
    rim_at = pl.multiple_of(jnp.where(odd == 1, mid + rows, SUBLANES), SUBLANES)
    is_edge = edge == 1

    high = 2 * mid + rows
    row = lax.broadcasted_iota(jnp.int32, (high, LANES), 0)
    outside = is_edge & (row >= rim_at) & (row < rim_at + rows)
    for stage in range(STAGES):
        coef[stage] = jnp.where(outside, 0.0, stage_scale(stage))

    def load(j, carry):
        col = columns(j)
        for t in row_groups(rows):
            src = pl.ds(t, SUBLANES)
            for part in range(2):
                field_a[j, part, pl.ds(mid + t, SUBLANES), :] = own_b[part, src, col]
                field_a[j, part, pl.ds(rim_at + t, SUBLANES), :] = jnp.where(
                    is_edge, 0.0, rim_b[part, src, col]
                )
            for k in range(sections):
                med[sec ^ k, j, pl.ds(mid + t, SUBLANES), :] = to_medium_term(
                    own_m[k][0, src, col]
                )
        at = 0
        for step, count in enumerate(rim_rows(rows, steps)):
            skip = jnp.where(odd == 1, 0, rows - count)
            for t in row_groups(count):
                to = pl.multiple_of(rim_at + skip + t, SUBLANES)
                med[first + step, j, pl.ds(to, SUBLANES), :] = to_medium_term(
                    rim_m[pl.ds(at + t, SUBLANES), col]
                )
            at += count
        return carry

    lax.fori_loop(0, chunks, load, 0)

    begin, end = field_a, field_b
    level = 0
    for step in range(steps):
        source = begin
        for stage in range(STAGES):
            if level > 0:
                edge_at = jnp.where(odd == 1, mid + rows - SUBLANES - level, mid + level)
                for j in range(chunks):
                    for part in range(2):
                        source[j, part, pl.ds(edge_at, SUBLANES), :] = edge_ref[
                            level - 1, j, part, :, :
                        ]
            level += 1
            target = (work_a, work_b, work_a, end)[stage]
            if level < depth:

                def store(j, block, part, here, value, target=target):
                    target[j, part, here, :] = value

            else:

                def store(j, block, part, here, value):
                    out_ref[part, pl.ds(SUBLANES * block, SUBLANES), columns(j)] = value

            run_stage(
                source, begin, med.at[first + step],
                jnp.where(odd == 1, mid + depth - level, mid + level - depth),
                rows // SUBLANES, chunks,
                lambda here, stage=stage: coef[stage, here, :], store,
            )
            source = target
        begin, end = end, begin


def rim_rows(rows, steps):
    return [
        -(-(STAGES * (steps - step) - 1) // SUBLANES) * SUBLANES for step in range(steps)
    ]


def pack_rim(own, sec, odd, rows, first, steps):
    parts = []
    for step, count in enumerate(rim_rows(rows, steps)):
        cut = lambda piece: (
            piece[0] if count == rows
            else jnp.where(odd == 1, piece[0, rows - count :], piece[0, :count])
        )
        part = cut(own[0])
        for k in range(1, len(own)):
            part = jnp.where((sec ^ k) == first + step, cut(own[k]), part)
        parts.append(part)
    return jnp.concatenate(parts, axis=0)


def per_device(beams, medium):
    sections, tiles = lax.axis_size("sec"), lax.axis_size("tile")
    _, rows, cols = medium.shape
    sec, tile = lax.axis_index("sec"), lax.axis_index("tile")
    odd = tile % 2
    place = jnp.stack(
        [sec, odd, ((tile == 0) | (tile == tiles - 1)).astype(jnp.int32)]
    ).astype(jnp.int32)
    swap = lambda value, pairs: lax.ppermute(value, AXES, pairs)
    pair, rim = pair_swap(sections, tiles), rim_swap(sections, tiles)

    own = [medium] + [
        swap(medium, sec_swap(sections, tiles, k)) for k in range(1, sections)
    ]
    pair_pieces = swap(jnp.concatenate(own, axis=0), pair)

    chunks = cols // LANES
    high = 2 * SUBLANES + 3 * rows
    smem = pl.BlockSpec(memory_space=pltpu.SMEM)
    whole = pl.BlockSpec(memory_space=pltpu.VMEM)
    buffers = [pltpu.VMEM((chunks, 2, high, LANES), jnp.float32)] * 4 + [
        pltpu.VMEM((sections, chunks, high, LANES), jnp.float32)
    ]
    params = pltpu.CompilerParams(vmem_limit_bytes=40 * 2**20)
    field = beams
    group = rows // STAGES
    for first in range(0, sections, group):
        steps = min(group, sections - first)
        depth = STAGES * steps
        pair_field, rim_field = swap(field, pair), swap(field, rim)
        *own, rim_field = lax.optimization_barrier((*own, rim_field))
        rim_pack = swap(pack_rim(own, sec, odd, rows, first, steps), rim)
        fixed = dict(sections=sections, first=first, rows=rows, cols=cols, steps=steps)
        own_field, pair_field, rim_field = (
            value.reshape(2, rows, cols) for value in (field, pair_field, rim_field)
        )
        work = 36 * 2 * SUBLANES * cols
        edges = pl.pallas_call(
            functools.partial(inner_kernel, **fixed),
            out_shape=jax.ShapeDtypeStruct(
                (depth - 1, chunks, 2, SUBLANES, LANES), jnp.float32
            ),
            in_specs=[smem] + [whole] * (4 + sections),
            out_specs=whole,
            scratch_shapes=buffers,
            compiler_params=params,
            cost_estimate=pl.CostEstimate(
                flops=10 * work, bytes_accessed=16 * work, transcendentals=0
            ),
            name="inner_rows",
        )(place, own_field, pair_field, rim_field, *own, pair_pieces)
        field = pl.pallas_call(
            functools.partial(outer_kernel, **fixed),
            out_shape=jax.ShapeDtypeStruct((2, rows, cols), jnp.float32),
            in_specs=[smem] + [whole] * (4 + sections),
            out_specs=whole,
            scratch_shapes=buffers + [pltpu.VMEM((STAGES, high, LANES), jnp.float32)],
            compiler_params=params,
            name="outer_rows",
        )(place, own_field, rim_field, *own, rim_pack, edges)[None]
    return field


def solution(mesh):
    placed = (P("sec", None, "tile", None), P("sec", "tile", None))
    return jax.shard_map(
        per_device,
        mesh=mesh,
        in_specs=placed,
        out_specs=P("sec", None, "tile", None),
        check_vma=False,
    )
```

time: 32.1 us -> 27.3 us (0.85)
  waiting for transfers between devices: 11.6 us -> 7.06 us
  starting transfers between devices: 11.9 us -> 8.23 us
  other arithmetic: 0.08 us -> 2.88 us
  Pallas kernels: 6.45 us -> 8.87 us
  local copies, waits for them, and re-layouts: 1.85 us -> 0.01 us
    ppermute x13 -> x7, waiting for transfers between devices: 11.6 us -> 7.06 us  [per_device(): swap = lambda value, pairs: lax.ppermute(value, AXES, pairs)]
    ppermute x13 -> x7, starting transfers between devices: 11.9 us -> 8.23 us  [per_device(): swap = lambda value, pairs: lax.ppermute(value, AXES, pairs)]
    pallas_call x1 -> x2, Pallas kernels: 6.45 us -> 8.87 us  [the longest x1 4.96 us: per_device(): pl.pallas_call(functools.partial(outer_kernel, **fixed), out_shape=jax.Sh...]
    unnamed x4, local copies, waits for them, and re-layouts: 1.85 us -> 0.01 us
    select_n x0 -> x3, other arithmetic: none -> 1.84 us  [pack_rim(): part = jnp.where(sec ^ k == first + step, cut(own[k]), part)]
    concatenate x0 -> x2, other arithmetic: none -> 0.97 us  [the longest x1 0.94 us: per_device(): pair_pieces = swap(jnp.concatenate(own, axis=0), pair)]
  transfers between devices with their start and end apart: 13 -> 7, of which waited for: 4 -> 5; matrix products, arithmetic and copies ran while one was open for 0% -> 11% of each run, Pallas kernels for 0% -> 14%
where the time goes in v2:
time: 27.3 us; the launch traced here: 27.1 us
  Pallas kernels  8.87 us (32%)
  starting transfers between devices  8.23 us (30%)
  waiting for transfers between devices  7.06 us (26%)
  other arithmetic  2.88 us (11%)
    ppermute x7, starting transfers between devices, per_device(): swap = lambda value, pairs: lax.ppermute(value, AXES, pairs)  8.23 us
    ppermute x7, waiting for transfers between devices, per_device(): swap = lambda value, pairs: lax.ppermute(value, AXES, pairs)  7.06 us
    pallas_call x1, Pallas kernels, per_device(): pl.pallas_call(functools.partial(outer_kernel, **fixed), out_shape=jax.Sh...  4.96 us
    pallas_call x1, Pallas kernels, per_device(): pl.pallas_call(functools.partial(inner_kernel, **fixed), out_shape=jax.Sh...  3.91 us
    select_n x3, other arithmetic, pack_rim(): part = jnp.where(sec ^ k == first + step, cut(own[k]), part)  1.84 us
    concatenate x1, other arithmetic, per_device(): pair_pieces = swap(jnp.concatenate(own, axis=0), pair)  0.94 us
  transfers between devices with their start and end apart: 7, of which 5 were waited for; matrix products, arithmetic and copies ran while one was open for 11% of the time, Pallas kernels for 14%

profile of v2, /device:TPU:0, one launch (start us, length us, event | category | flops | bytes accessed | tf_op | source)
XLA Modules:
  0.0 27.1 jit_solution(11648550257940679174)
XLA Ops:
  0.0 0.0 copy-start
  0.0 0.0 copy-start.1
  0.0 2.9 %collective-permute-start = (f32[1,16,2048]{2,1,0:T(8,128)}, f32[1,16,2048]{2,1,0:T(8,128)S(1)}, u32[]{:S(2)}, u32[]{:S(2)}) collective-permute-start(f32[1,16,2048]{2,1,0:T(8,128)} %refs_2_), channel_id=1, source_target_pairs={{0,8},{1,9},{2,10},{3,11},{4,12},{5,13},{6,14},{7,15},{8,0},{9,1},... | collective-permute-start | bytes 393224 | tf_op jit(solution)/shard_map/ppermute | solution.py:248
  2.9 1.5 %collective-permute-start.1 = (f32[1,16,2048]{2,1,0:T(8,128)}, f32[1,16,2048]{2,1,0:T(8,128)S(1)}, u32[]{:S(2)}, u32[]{:S(2)}) collective-permute-start(f32[1,16,2048]{2,1,0:T(8,128)} %refs_2_), channel_id=1, source_target_pairs={{0,16},{1,17},{2,18},{3,19},{4,20},{5,21},{6,22},{7,23},{8,24},{9,... | collective-permute-start | bytes 393224 | tf_op jit(solution)/shard_map/ppermute | solution.py:248
  4.5 0.0 collective-permute-start.2
  4.5 2.0 %collective-permute-start.3 = (f32[1,2,16,2048]{3,2,1,0:T(8,128)}, f32[1,2,16,2048]{3,2,1,0:T(8,128)S(1)}, u32[]{:S(2)}, u32[]{:S(2)}) collective-permute-start(f32[1,2,16,2048]{3,2,1,0:T(8,128)} %param.2), channel_id=1, source_target_pairs={{0,8},{1,2},{2,1},{3,4},{4,3},{5,6},{6,5},{7,15},{8,0},{9,10},{10,... | collective-permute-start | bytes 786440 | tf_op jit(solution)/shard_map/ppermute | solution.py:248
  6.4 0.7 %collective-permute-done.refs_4_.refs_3_ = f32[1,16,2048]{2,1,0:T(8,128)S(1)} collective-permute-done((f32[1,16,2048]{2,1,0:T(8,128)}, f32[1,16,2048]{2,1,0:T(8,128)S(1)}, u32[]{:S(2)}, u32[]{:S(2)}) %collective-permute-start) | collective-permute-done | bytes 131104 | tf_op jit(solution)/shard_map/ppermute | solution.py:248
  7.2 3.8 %collective-permute-done.1.refs_5_.refs_4_ = f32[1,16,2048]{2,1,0:T(8,128)S(1)} collective-permute-done((f32[1,16,2048]{2,1,0:T(8,128)}, f32[1,16,2048]{2,1,0:T(8,128)S(1)}, u32[]{:S(2)}, u32[]{:S(2)}) %collective-permute-start.1) | collective-permute-done | bytes 131104 | tf_op jit(solution)/shard_map/ppermute | solution.py:248
  10.9 0.0 collective-permute-done.2.refs_6_.refs_5_
  10.9 0.9 %pad_maximum_fusion = f32[4,16,2048]{2,1,0:T(8,128)S(1)} fusion(f32[1,16,2048]{2,1,0:T(8,128)S(1)} %collective-permute-done.2.refs_6_.refs_5_, f32[1,16,2048]{2,1,0:T(8,128)S(1)} %collective-permute-done.1.refs_5_.refs_4_, f32[1,16,2048]{2,1,0:T(8,128)S(1)} %collective-permute-done.refs_4_.refs_3_, f32[1,16,2048]{2,1,0:T(8,128)} %refs_2_), kind=kLoop, calls=%fused_computation | loop fusion | flops 393216 | bytes 1048576 | tf_op jit(solution)/shard_map/concatenate | solution.py:254
  11.9 0.1 collective-permute-start.6
  12.0 0.4 %collective-permute-done.3 = f32[1,2,16,2048]{3,2,1,0:T(8,128)S(1)} collective-permute-done((f32[1,2,16,2048]{3,2,1,0:T(8,128)}, f32[1,2,16,2048]{3,2,1,0:T(8,128)S(1)}, u32[]{:S(2)}, u32[]{:S(2)}) %collective-permute-start.3) | collective-permute-done | bytes 262176 | tf_op jit(solution)/shard_map/ppermute | solution.py:248
  12.4 0.9 %select_bitcast_fusion.3 = f32[8,2048]{1,0:T(8,128)S(1)} fusion(pred[]{:T(512)S(6)} %eq.65, pred[]{:T(512)S(6)} %eq.64, pred[]{:T(512)S(6)} %eq.62, f32[1,16,2048]{2,1,0:T(8,128)S(1)} %collective-permute-done.2.refs_6_.refs_5_, pred[]{:T(512)S(6)} %eq.63, f32[1,16,2048]{2,1,0:T(8,128)S(1)} %collective-permute-done.1.refs_5_.refs_4_, ...), kind=kLoop, calls=%fused_computation.5 | loop fusion | flops 114688 | bytes 589828 | tf_op jit(solution)/shard_map/jit(_where)/select_n | solution.py:235
  13.3 0.9 %select_bitcast_fusion.2 = f32[8,2048]{1,0:T(8,128)S(1)} fusion(pred[]{:T(512)S(6)} %eq.68, pred[]{:T(512)S(6)} %eq.67, pred[]{:T(512)S(6)} %eq.66, f32[1,16,2048]{2,1,0:T(8,128)S(1)} %collective-permute-done.2.refs_6_.refs_5_, pred[]{:T(512)S(6)} %eq.63, f32[1,16,2048]{2,1,0:T(8,128)S(1)} %collective-permute-done.1.refs_5_.refs_4_, ...), kind=kLoop, calls=%fused_computation.4 | loop fusion | flops 114688 | bytes 589828 | tf_op jit(solution)/shard_map/jit(_where)/select_n | solution.py:235
  14.2 0.0 copy-done
  14.3 1.7 %collective-permute-start.4 = (f32[48,2048]{1,0:T(8,128)S(1)}, f32[48,2048]{1,0:T(8,128)S(1)}, u32[]{:S(2)}, u32[]{:S(2)}) collective-permute-start(f32[48,2048]{1,0:T(8,128)S(1)} %pad_maximum_fusion.1), channel_id=1, source_target_pairs={{0,8},{1,2},{2,1},{3,4},{4,3},{5,6},{6,5},{7,15},{8,0},{9,10},{10,... | collective-permute-start | bytes 1179656 | tf_op jit(solution)/shard_map/ppermute | solution.py:248
  16.0 0.0 copy-done.1
  16.0 0.0 collective-permute-start.5
  16.0 0.1 pad_add_fusion.place_ref
  16.1 1.5 %collective-permute-done.5 = f32[1,2,16,2048]{3,2,1,0:T(8,128)S(1)} collective-permute-done((f32[1,2,16,2048]{3,2,1,0:T(8,128)S(1)}, f32[1,2,16,2048]{3,2,1,0:T(8,128)S(1)}, u32[]{:S(2)}, u32[]{:S(2)}) %collective-permute-start.5) | collective-permute-done | bytes 262176 | tf_op jit(solution)/shard_map/ppermute | solution.py:248
  17.6 0.0 collective-permute-done.6.refs_7_
  17.6 3.9 %inner_rows.1.refs_7_ = f32[15,16,2,8,128]{4,3,2,1,0:T(8,128)S(1)} custom-call(s32[3]{0:T(128)S(1)} %pad_add_fusion.place_ref, f32[2,16,2048]{2,1,0:T(8,128)S(1)} %bitcast.15, f32[2,16,2048]{2,1,0:T(8,128)S(1)} %bitcast.19, f32[2,16,2048]{2,1,0:T(8,128)S(1)} %bitcast.17, f32[1,16,2048]{2,1,0:T(8,128)S(1)} %copy-done, ...), custom_call_target="tpu_custom_call" | custom-call | flops 11796480 | bytes 18874368 | tf_op jit(solution)/shard_map/inner_rows/pallas_call | solution.py:277
  21.5 0.7 %collective-permute-done.4.refs_6_ = f32[48,2048]{1,0:T(8,128)S(1)} collective-permute-done((f32[48,2048]{1,0:T(8,128)S(1)}, f32[48,2048]{1,0:T(8,128)S(1)}, u32[]{:S(2)}, u32[]{:S(2)}) %collective-permute-start.4) | collective-permute-done | bytes 393248 | tf_op jit(solution)/shard_map/ppermute | solution.py:248
  22.1 5.0 %outer_rows.1 = f32[2,16,2048]{2,1,0:T(8,128)} custom-call(s32[3]{0:T(128)S(1)} %pad_add_fusion.place_ref, f32[2,16,2048]{2,1,0:T(8,128)S(1)} %bitcast.16, f32[2,16,2048]{2,1,0:T(8,128)S(1)} %bitcast.18, f32[1,16,2048]{2,1,0:T(8,128)S(1)} %copy-done, f32[1,16,2048]{2,1,0:T(8,128)S(1)} %collective-permute-done.refs_4_.refs_3_, ...), custom_call_target="tpu_custom_call" | custom-call | tf_op jit(solution)/shard_map/outer_rows/pallas_call | solution.py:291
  (2 shorter events, 0.1 us)
Async XLA Ops:
  0.0 14.2 %copy-start = (f32[1,16,2048]{2,1,0:T(8,128)S(1)}, f32[1,16,2048]{2,1,0:T(8,128)}, u32[]{:S(2)}) copy-start(f32[1,16,2048]{2,1,0:T(8,128)} %refs_2_) | copy-start | bytes 393220
  0.0 16.0 %copy-start.1 = (f32[1,2,16,2048]{3,2,1,0:T(8,128)S(1)}, f32[1,2,16,2048]{3,2,1,0:T(8,128)}, u32[]{:S(2)}) copy-start(f32[1,2,16,2048]{3,2,1,0:T(8,128)} %param.2) | copy-start | bytes 786436
  0.0 7.2 %collective-permute-start = (f32[1,16,2048]{2,1,0:T(8,128)}, f32[1,16,2048]{2,1,0:T(8,128)S(1)}, u32[]{:S(2)}, u32[]{:S(2)}) collective-permute-start(f32[1,16,2048]{2,1,0:T(8,128)} %refs_2_), channel_id=1, source_target_pairs={{0,8},{1,9},{2,10},{3,11},{4,12},{5,13},{6,14},{7,15},{8,0},{9,1},... | collective-permute-start | bytes 393224 | tf_op jit(solution)/shard_map/ppermute | solution.py:248
  2.9 8.0 %collective-permute-start.1 = (f32[1,16,2048]{2,1,0:T(8,128)}, f32[1,16,2048]{2,1,0:T(8,128)S(1)}, u32[]{:S(2)}, u32[]{:S(2)}) collective-permute-start(f32[1,16,2048]{2,1,0:T(8,128)} %refs_2_), channel_id=1, source_target_pairs={{0,16},{1,17},{2,18},{3,19},{4,20},{5,21},{6,22},{7,23},{8,24},{9,... | collective-permute-start | bytes 393224 | tf_op jit(solution)/shard_map/ppermute | solution.py:248
  4.5 6.5 %collective-permute-start.2 = (f32[1,16,2048]{2,1,0:T(8,128)}, f32[1,16,2048]{2,1,0:T(8,128)S(1)}, u32[]{:S(2)}, u32[]{:S(2)}) collective-permute-start(f32[1,16,2048]{2,1,0:T(8,128)} %refs_2_), channel_id=1, source_target_pairs={{0,24},{1,25},{2,26},{3,27},{4,28},{5,29},{6,30},{7,31},{8,16},{9,... | collective-permute-start | bytes 393224 | tf_op jit(solution)/shard_map/ppermute | solution.py:248
  4.5 7.9 %collective-permute-start.3 = (f32[1,2,16,2048]{3,2,1,0:T(8,128)}, f32[1,2,16,2048]{3,2,1,0:T(8,128)S(1)}, u32[]{:S(2)}, u32[]{:S(2)}) collective-permute-start(f32[1,2,16,2048]{3,2,1,0:T(8,128)} %param.2), channel_id=1, source_target_pairs={{0,8},{1,2},{2,1},{3,4},{4,3},{5,6},{6,5},{7,15},{8,0},{9,10},{10,... | collective-permute-start | bytes 786440 | tf_op jit(solution)/shard_map/ppermute | solution.py:248
  11.9 5.7 %collective-permute-start.6 = (f32[4,16,2048]{2,1,0:T(8,128)S(1)}, f32[4,16,2048]{2,1,0:T(8,128)S(1)}, u32[]{:S(2)}, u32[]{:S(2)}) collective-permute-start(f32[4,16,2048]{2,1,0:T(8,128)S(1)} %pad_maximum_fusion), channel_id=1, source_target_pairs={{0,1},{1,0},{2,3},{3,2},{4,5},{5,4},{6,7},{7,6},{8,9},{9,8},{10,11... | collective-permute-start | bytes 1572872 | tf_op jit(solution)/shard_map/ppermute | solution.py:248
  14.3 7.8 %collective-permute-start.4 = (f32[48,2048]{1,0:T(8,128)S(1)}, f32[48,2048]{1,0:T(8,128)S(1)}, u32[]{:S(2)}, u32[]{:S(2)}) collective-permute-start(f32[48,2048]{1,0:T(8,128)S(1)} %pad_maximum_fusion.1), channel_id=1, source_target_pairs={{0,8},{1,2},{2,1},{3,4},{4,3},{5,6},{6,5},{7,15},{8,0},{9,10},{10,... | collective-permute-start | bytes 1179656 | tf_op jit(solution)/shard_map/ppermute | solution.py:248
  16.0 1.5 %collective-permute-start.5 = (f32[1,2,16,2048]{3,2,1,0:T(8,128)S(1)}, f32[1,2,16,2048]{3,2,1,0:T(8,128)S(1)}, u32[]{:S(2)}, u32[]{:S(2)}) collective-permute-start(f32[1,2,16,2048]{3,2,1,0:T(8,128)S(1)} %copy-done.1), channel_id=1, source_target_pairs={{0,1},{1,0},{2,3},{3,2},{4,5},{5,4},{6,7},{7,6},{8,9},{9,8},{10,11... | collective-permute-start | bytes 786440 | tf_op jit(solution)/shard_map/ppermute | solution.py:248

commit v3 on v2

v3 whole, which is shorter than its diff:
```python
import functools

import jax
import jax.numpy as jnp
from jax import lax
from jax.experimental import pallas as pl
from jax.experimental.pallas import tpu as pltpu
from jax.sharding import PartitionSpec as P

AXES = ("sec", "tile")
LANES = 128
SUBLANES = 8
STAGES = 4
OUT_PARTS = 4

diffract_coef = 0.5
step_length = 0.65


def sec_swap(sec, tiles, k):
    return [(s * tiles + t, (s ^ k) * tiles + t) for s in range(sec) for t in range(tiles)]


def pair_swap(sec, tiles):
    return [(s * tiles + t, s * tiles + (t ^ 1)) for s in range(sec) for t in range(tiles)]


def rim_swap(sec, tiles):
    out = []
    for s in range(sec):
        for t in range(tiles):
            if 0 < t < tiles - 1:
                out.append((s * tiles + t, s * tiles + ((t + 1) ^ 1) - 1))
            else:
                out.append((s * tiles + t, (s ^ 1) * tiles + t))
    return out


def stage_scale(stage):
    return diffract_coef * step_length / (STAGES - stage)


def run_stage(source, begin, med, start, blocks, chunks, scale_of, store):
    lane = lax.broadcasted_iota(jnp.int32, (SUBLANES, LANES), 1)
    low_lane, high_lane = lane == 0, lane == LANES - 1
    for j in range(chunks):
        for block in range(blocks):
            at = start + SUBLANES * block
            here = pl.ds(at, SUBLANES)
            m = med[j, here, :]
            g = scale_of(here)
            drive = []
            for part in range(2):
                w = source[j, part, here, :]
                rows_sum = (
                    source[j, part, pl.ds(at - 1, SUBLANES), :]
                    + source[j, part, pl.ds(at + 1, SUBLANES), :]
                )
                before = source[j - 1, part, here, :] if j > 0 else jnp.zeros_like(w)
                after = source[j + 1, part, here, :] if j + 1 < chunks else jnp.zeros_like(w)
                left = pltpu.roll(jnp.where(high_lane, before, w), 1, 1)
                right = pltpu.roll(jnp.where(low_lane, after, w), LANES - 1, 1)
                drive.append(g * (rows_sum + (left + right) + m * w))
            store(j, block, 0, here, begin[j, 0, here, :] - drive[1])
            store(j, block, 1, here, begin[j, 1, here, :] + drive[0])


def row_groups(rows):
    return range(0, rows, SUBLANES)


def columns(j):
    return pl.ds(j * LANES, LANES)


def to_medium_term(value):
    return value * (1.0 / diffract_coef) - 4.0


def by_side(odd, body):
    pl.when(odd == 1)(functools.partial(body, True))
    pl.when(odd == 0)(functools.partial(body, False))


def inner_kernel(place_ref, *refs, sections, first, rows, cols, steps):
    own_b, pair_b = refs[:2]
    own_m = refs[2 : 2 + sections]
    pair_m = refs[2 + sections]
    edge_ref = refs[3 + sections]
    field_a, field_b, work_a, work_b, med = refs[4 + sections :]
    sec, odd = place_ref[0], place_ref[1]
    chunks = cols // LANES
    depth = STAGES * steps
    mid = SUBLANES + rows

    def run(is_odd):
        low = SUBLANES if is_odd else mid
        pair_at = SUBLANES if is_odd else mid + rows
        for j in range(chunks):
            col = columns(j)
            for t in row_groups(rows):
                src = pl.ds(t, SUBLANES)
                for part in range(2):
                    field_a[j, part, pl.ds(mid + t, SUBLANES), :] = own_b[part, src, col]
                    field_a[j, part, pl.ds(pair_at + t, SUBLANES), :] = pair_b[part, src, col]
                for k in range(sections):
                    slot = sec ^ k
                    med[slot, j, pl.ds(mid + t, SUBLANES), :] = to_medium_term(
                        own_m[k][0, src, col]
                    )
                    med[slot, j, pl.ds(pair_at + t, SUBLANES), :] = to_medium_term(
                        pair_m[k, src, col]
                    )
        begin, end = field_a, field_b
        level = 0
        for step in range(steps):
            source = begin
            for stage in range(STAGES):
                level += 1
                if level == depth:
                    break
                target = (work_a, work_b, work_a, end)[stage]

                def store(j, block, part, here, value, target=target):
                    target[j, part, here, :] = value

                run_stage(
                    source, begin, med.at[first + step], low + level,
                    -(-(2 * (rows - level)) // SUBLANES), chunks,
                    lambda here, stage=stage: stage_scale(stage), store,
                )
                edge_at = mid + rows - SUBLANES - level if is_odd else mid + level
                for j in range(chunks):
                    for part in range(2):
                        edge_ref[level - 1, j, part, :, :] = target[
                            j, part, pl.ds(edge_at, SUBLANES), :
                        ]
                source = target
            begin, end = end, begin

    by_side(odd, run)


def outer_kernel(place_ref, *refs, sections, first, rows, cols, steps):
    own_b, rim_b = refs[:2]
    own_m = refs[2 : 2 + sections]
    rim_m, edge_ref, out_ref, levels, med, coef, result, sems = refs[2 + sections :]
    sec, odd, edge = place_ref[0], place_ref[1], place_ref[2]
    chunks = cols // LANES
    depth = STAGES * steps
    mid = SUBLANES + rows
    is_edge = edge == 1
    parts = sems.shape[0]
    per_part = chunks // parts

    def run(is_odd):
        rim_at = mid + rows if is_odd else SUBLANES
        row = lax.broadcasted_iota(jnp.int32, coef.shape[1:], 0)
        outside = is_edge & (row >= rim_at) & (row < rim_at + rows)
        for stage in range(STAGES):
            coef[stage] = jnp.where(outside, 0.0, stage_scale(stage))
        for j in range(chunks):
            col = columns(j)
            for t in row_groups(rows):
                src = pl.ds(t, SUBLANES)
                for part in range(2):
                    levels[0, j, part, pl.ds(rim_at + t, SUBLANES), :] = jnp.where(
                        is_edge, 0.0, rim_b[part, src, col]
                    )
            near = rows - SUBLANES if is_odd else 0
            for part in range(2):
                levels[0, j, part, pl.ds(mid + near, SUBLANES), :] = own_b[
                    part, pl.ds(near, SUBLANES), col
                ]
            for k in range(sections):
                for t in row_groups(rows):
                    med[sec ^ k, j, pl.ds(mid + t, SUBLANES), :] = to_medium_term(
                        own_m[k][0, pl.ds(t, SUBLANES), col]
                    )
            at = 0
            for step, count in enumerate(rim_rows(rows, steps)):
                over = -count % SUBLANES
                there = mid + rows if is_odd else mid - count - over
                for t in row_groups(count):
                    here = at + t - (0 if is_odd else over)
                    if is_odd and here + SUBLANES > rim_m.shape[1]:
                        size = rim_m.shape[1] - here
                    else:
                        size = SUBLANES
                    med[first + step, j, pl.ds(there + t, size), :] = to_medium_term(
                        rim_m[j, pl.ds(here, size), :]
                    )
                at += count
            for level in range(1, depth):
                edge_at = mid + rows - SUBLANES - level if is_odd else mid + level
                for part in range(2):
                    levels[level, j, part, pl.ds(edge_at, SUBLANES), :] = edge_ref[
                        level - 1, j, part, :, :
                    ]

        copies = [
            pltpu.make_async_copy(
                result.at[:, :, pl.ds(p * per_part * LANES, per_part * LANES)],
                out_ref.at[:, :, pl.ds(p * per_part * LANES, per_part * LANES)],
                sems.at[p],
            )
            for p in range(parts)
        ]
        level = 0
        for step in range(steps):
            begin = levels.at[level]
            for stage in range(STAGES):
                level += 1

                def store(j, block, part, here, value, level=level):
                    if level < depth:
                        levels[level, j, part, here, :] = value
                        return
                    result[part, pl.ds(SUBLANES * block, SUBLANES), columns(j)] = value
                    if part == 1 and block + 1 == rows // SUBLANES and (j + 1) % per_part == 0:
                        copies[j // per_part].start()

                run_stage(
                    levels.at[level - 1], begin, med.at[first + step],
                    mid + depth - level if is_odd else mid + level - depth,
                    rows // SUBLANES, chunks,
                    lambda here, stage=stage: coef[stage, here, :], store,
                )
        for copy in copies:
            copy.wait()

    by_side(odd, run)


def rim_rows(rows, steps):
    return [STAGES * (steps - step) for step in range(steps)]


def pack_kernel(place_ref, *refs, sections, first, rows, cols, steps):
    own_m, rim_out = refs[:sections], refs[sections]
    sec, odd = place_ref[0], place_ref[1]
    chunks = cols // LANES

    def pack(k, at, lo, hi):
        def body():
            for t in row_groups(rows):
                cut_lo, cut_hi = max(lo, t), min(hi, t + SUBLANES)
                if cut_lo < cut_hi:
                    for j in range(chunks):
                        rim_out[j, pl.ds(at + cut_lo - lo, cut_hi - cut_lo), :] = own_m[k][
                            0, pl.ds(cut_lo, cut_hi - cut_lo), columns(j)
                        ]

        return body

    at = 0
    for step, count in enumerate(rim_rows(rows, steps)):
        for k in range(sections):
            mine = (sec ^ k) == first + step
            pl.when(mine & (odd == 1))(pack(k, at, rows - count, rows))
            pl.when(mine & (odd == 0))(pack(k, at, 0, count))
        at += count


def load_kernel(field_ref, medium_ref, field_out, medium_out, field_sem, medium_sem):
    copies = (
        pltpu.make_async_copy(medium_ref, medium_out, medium_sem),
        pltpu.make_async_copy(field_ref, field_out, field_sem),
    )
    for copy in copies:
        copy.start()
    for copy in copies:
        copy.wait()


def per_device(beams, medium):
    sections, tiles = lax.axis_size("sec"), lax.axis_size("tile")
    _, rows, cols = medium.shape
    sec, tile = lax.axis_index("sec"), lax.axis_index("tile")
    odd = tile % 2
    place = jnp.stack(
        [sec, odd, ((tile == 0) | (tile == tiles - 1)).astype(jnp.int32)]
    ).astype(jnp.int32)
    swap = lambda value, pairs: lax.ppermute(value, AXES, pairs)
    pair, rim = pair_swap(sections, tiles), rim_swap(sections, tiles)

    far = [swap(medium, sec_swap(sections, tiles, k)) for k in range(1, sections)]
    chunks = cols // LANES
    high = 2 * SUBLANES + 3 * rows
    smem = pl.BlockSpec(memory_space=pltpu.SMEM)
    whole = pl.BlockSpec(memory_space=pltpu.VMEM)
    buffers = [pltpu.VMEM((chunks, 2, high, LANES), jnp.float32)] * 4 + [
        pltpu.VMEM((sections, chunks, high, LANES), jnp.float32)
    ]
    params = pltpu.CompilerParams(vmem_limit_bytes=40 * 2**20)
    field, medium = pl.pallas_call(
        load_kernel,
        out_shape=(
            pltpu.VMEM(beams.shape, beams.dtype),
            pltpu.VMEM(medium.shape, medium.dtype),
        ),
        in_specs=[pl.BlockSpec(memory_space=pl.ANY)] * 2,
        out_specs=(whole, whole),
        scratch_shapes=[pltpu.SemaphoreType.DMA(())] * 2,
        cost_estimate=pl.CostEstimate(flops=0, bytes_accessed=2**21, transcendentals=0),
        name="load_arguments",
    )(beams, medium)
    own = [medium] + far
    group = rows // STAGES
    for first in range(0, sections, group):
        steps = min(group, sections - first)
        depth = STAGES * steps
        sent = field if first > 0 else beams
        pair_field, rim_field = swap(sent, pair), swap(sent, rim)
        *own, field = lax.optimization_barrier((*own, field))
        fixed = dict(sections=sections, first=first, rows=rows, cols=cols, steps=steps)
        pair_pack = jnp.concatenate(own, axis=0)
        rim_pack = pl.pallas_call(
            functools.partial(pack_kernel, **fixed),
            out_shape=jax.ShapeDtypeStruct(
                (chunks, sum(rim_rows(rows, steps)), LANES), jnp.float32
            ),
            in_specs=[smem] + [whole] * sections,
            out_specs=whole,
            compiler_params=params,
            name="pack_rows",
        )(place, *own)
        rim_pack, pair_pack = swap(rim_pack, rim), swap(pair_pack, pair)
        own_field, pair_field, rim_field = (
            value.reshape(2, rows, cols) for value in (field, pair_field, rim_field)
        )
        work = 36 * 2 * SUBLANES * cols
        edges = pl.pallas_call(
            functools.partial(inner_kernel, **fixed),
            out_shape=jax.ShapeDtypeStruct(
                (depth - 1, chunks, 2, SUBLANES, LANES), jnp.float32
            ),
            in_specs=[smem] + [whole] * (3 + sections),
            out_specs=whole,
            scratch_shapes=buffers,
            compiler_params=params,
            cost_estimate=pl.CostEstimate(
                flops=10 * work, bytes_accessed=16 * work, transcendentals=0
            ),
            name="inner_rows",
        )(place, own_field, pair_field, *own, pair_pack)
        field = pl.pallas_call(
            functools.partial(outer_kernel, **fixed),
            out_shape=jax.ShapeDtypeStruct((2, rows, cols), jnp.float32),
            in_specs=[smem] + [whole] * (4 + sections),
            out_specs=pl.BlockSpec(memory_space=pl.ANY),
            scratch_shapes=[
                pltpu.VMEM((depth, chunks, 2, high, LANES), jnp.float32),
                pltpu.VMEM((sections, chunks, high, LANES), jnp.float32),
                pltpu.VMEM((STAGES, high, LANES), jnp.float32),
                pltpu.VMEM((2, rows, cols), jnp.float32),
                pltpu.SemaphoreType.DMA((OUT_PARTS,)),
            ],
            compiler_params=params,
            name="outer_rows",
        )(place, own_field, rim_field, *own, rim_pack, edges)[None]
    return field


def solution(mesh):
    placed = (P("sec", None, "tile", None), P("sec", "tile", None))
    return jax.shard_map(
        per_device,
        mesh=mesh,
        in_specs=placed,
        out_specs=P("sec", None, "tile", None),
        check_vma=False,
    )
```

time: 27.3 us -> 25.6 us (0.938)
  other arithmetic: 2.88 us -> 0.11 us
  waiting for transfers between devices: 7.06 us -> 8.76 us
  starting transfers between devices: 8.23 us -> 7.51 us
    select_n x3 -> x0, other arithmetic: 1.84 us -> none  [pack_rim(): part = jnp.where(sec ^ k == first + step, cut(own[k]), part)]
    pallas_call x0 -> x2, Pallas kernels: none -> 1.75 us  [the longest x1 1.03 us: per_device(): pl.pallas_call(load_kernel, out_shape=(pltpu.VMEM(beams.shape, beams.dtyp...]
    ppermute x7, waiting for transfers between devices: 7.06 us -> 8.76 us  [per_device(): swap = lambda value, pairs: lax.ppermute(value, AXES, pairs)]
    pallas_call x1, Pallas kernels: 4.96 us -> 3.65 us  [per_device(): pl.pallas_call(functools.partial(outer_kernel, **fixed), out_shape=jax.Sh...]
    concatenate x2 -> x1, other arithmetic: 0.97 us -> 0.03 us  [per_device(): pair_pack = jnp.concatenate(own, axis=0)]
    ppermute x7, starting transfers between devices: 8.23 us -> 7.51 us  [per_device(): swap = lambda value, pairs: lax.ppermute(value, AXES, pairs)]
    pallas_call x1, Pallas kernels: 3.91 us -> 3.63 us  [per_device(): pl.pallas_call(functools.partial(inner_kernel, **fixed), out_shape=jax.Sh...]
  transfers between devices with their start and end apart: 7 -> 7, of which waited for: 5 -> 3; matrix products, arithmetic and copies ran while one was open for 11% -> 0% of each run, Pallas kernels for 14% -> 21%
where the time goes in v3:
time: 25.6 us; the launch traced here: 25.5 us
  Pallas kernels  9.02 us (35%)
  waiting for transfers between devices  8.76 us (34%)
  starting transfers between devices  7.51 us (29%)
    ppermute x7, waiting for transfers between devices, per_device(): swap = lambda value, pairs: lax.ppermute(value, AXES, pairs)  8.76 us
    ppermute x7, starting transfers between devices, per_device(): swap = lambda value, pairs: lax.ppermute(value, AXES, pairs)  7.51 us
    pallas_call x1, Pallas kernels, per_device(): pl.pallas_call(functools.partial(outer_kernel, **fixed), out_shape=jax.Sh...  3.65 us
    pallas_call x1, Pallas kernels, per_device(): pl.pallas_call(functools.partial(inner_kernel, **fixed), out_shape=jax.Sh...  3.63 us
    pallas_call x1, Pallas kernels, per_device(): pl.pallas_call(load_kernel, out_shape=(pltpu.VMEM(beams.shape, beams.dtyp...  1.03 us
    pallas_call x1, Pallas kernels, per_device(): pl.pallas_call(functools.partial(pack_kernel, **fixed), out_shape=jax.Sha...  0.72 us
  transfers between devices with their start and end apart: 7, of which 3 were waited for; matrix products, arithmetic and copies ran while one was open for 0% of the time, Pallas kernels for 21%

profile of v3, /device:TPU:0, one launch (start us, length us, event | category | flops | bytes accessed | tf_op | source)
XLA Modules:
  0.0 25.5 jit_solution(13990764683676355523)
XLA Ops:
  0.0 0.0 copy-start
  0.0 2.9 %collective-permute-start = (f32[1,16,2048]{2,1,0:T(8,128)}, f32[1,16,2048]{2,1,0:T(8,128)S(1)}, u32[]{:S(2)}, u32[]{:S(2)}) collective-permute-start(f32[1,16,2048]{2,1,0:T(8,128)} %medium_ref.1), channel_id=1, source_target_pairs={{0,8},{1,9},{2,10},{3,11},{4,12},{5,13},{6,14},{7,15},{8,0},{9,1},... | collective-permute-start | bytes 393224 | tf_op jit(solution)/shard_map/ppermute | solution.py:284
  2.9 1.5 %collective-permute-start.1 = (f32[1,16,2048]{2,1,0:T(8,128)}, f32[1,16,2048]{2,1,0:T(8,128)S(1)}, u32[]{:S(2)}, u32[]{:S(2)}) collective-permute-start(f32[1,16,2048]{2,1,0:T(8,128)} %medium_ref.1), channel_id=1, source_target_pairs={{0,16},{1,17},{2,18},{3,19},{4,20},{5,21},{6,22},{7,23},{8,24},{9,... | collective-permute-start | bytes 393224 | tf_op jit(solution)/shard_map/ppermute | solution.py:284
  4.5 0.0 collective-permute-start.2
  4.5 1.0 %load_arguments.1 = (f32[1,2,16,2048]{3,2,1,0:T(8,128)S(1)}, f32[1,16,2048]{2,1,0:T(8,128)S(1)}) custom-call(f32[1,2,16,2048]{3,2,1,0:T(8,128)} %field_ref.1, f32[1,16,2048]{2,1,0:T(8,128)} %medium_ref.1), custom_call_target="tpu_custom_call" | custom-call | bytes 2097152 | tf_op jit(solution)/shard_map/load_arguments/pallas_call | solution.py:296
  5.5 1.7 %collective-permute-done.refs_1_.refs_3_ = f32[1,16,2048]{2,1,0:T(8,128)S(1)} collective-permute-done((f32[1,16,2048]{2,1,0:T(8,128)}, f32[1,16,2048]{2,1,0:T(8,128)S(1)}, u32[]{:S(2)}, u32[]{:S(2)}) %collective-permute-start) | collective-permute-done | bytes 131104 | tf_op jit(solution)/shard_map/ppermute | solution.py:284
  7.2 3.8 %collective-permute-done.1.refs_2_.refs_4_ = f32[1,16,2048]{2,1,0:T(8,128)S(1)} collective-permute-done((f32[1,16,2048]{2,1,0:T(8,128)}, f32[1,16,2048]{2,1,0:T(8,128)S(1)}, u32[]{:S(2)}, u32[]{:S(2)}) %collective-permute-start.1) | collective-permute-done | bytes 131104 | tf_op jit(solution)/shard_map/ppermute | solution.py:284
  10.9 0.0 collective-permute-done.2.refs_3_.refs_5_
  11.0 0.1 collective-permute-start.6
  11.1 0.1 pad_add_fusion.place_ref
  11.1 0.7 %pack_rows.1 = f32[16,40,128]{2,1,0:T(8,128)S(1)} custom-call(s32[3]{0:T(128)S(1)} %pad_add_fusion.place_ref, f32[1,16,2048]{2,1,0:T(8,128)S(1)} %get-tuple-element.15.refs_0_.refs_2_, f32[1,16,2048]{2,1,0:T(8,128)S(1)} %collective-permute-done.refs_1_.refs_3_, f32[1,16,2048]{2,1,0:T(8,128)S(1)} %collective-permute-done.1.refs_2_.refs_4_, ...), custom_call_target="tpu_custom_call" | custom-call | tf_op jit(solution)/shard_map/pack_rows/pallas_call | solution.py:318
  11.9 1.3 %collective-permute-start.4 = (f32[16,40,128]{2,1,0:T(8,128)S(1)}, f32[16,40,128]{2,1,0:T(8,128)S(1)}, u32[]{:S(2)}, u32[]{:S(2)}) collective-permute-start(f32[16,40,128]{2,1,0:T(8,128)S(1)} %pack_rows.1), channel_id=1, source_target_pairs={{0,8},{1,2},{2,1},{3,4},{4,3},{5,6},{6,5},{7,15},{8,0},{9,10},{10,... | collective-permute-start | bytes 983048 | tf_op jit(solution)/shard_map/ppermute | solution.py:284
  13.2 0.0 copy-done
  13.2 0.5 %collective-permute-start.5 = (f32[1,2,16,2048]{3,2,1,0:T(8,128)S(1)}, f32[1,2,16,2048]{3,2,1,0:T(8,128)S(1)}, u32[]{:S(2)}, u32[]{:S(2)}) collective-permute-start(f32[1,2,16,2048]{3,2,1,0:T(8,128)S(1)} %copy-done), channel_id=1, source_target_pairs={{0,1},{1,0},{2,3},{3,2},{4,5},{5,4},{6,7},{7,6},{8,9},{9,8},{10,11... | collective-permute-start | bytes 786440 | tf_op jit(solution)/shard_map/ppermute | solution.py:284
  13.6 1.2 %collective-permute-start.3 = (f32[1,2,16,2048]{3,2,1,0:T(8,128)S(1)}, f32[1,2,16,2048]{3,2,1,0:T(8,128)S(1)}, u32[]{:S(2)}, u32[]{:S(2)}) collective-permute-start(f32[1,2,16,2048]{3,2,1,0:T(8,128)S(1)} %copy-done), channel_id=1, source_target_pairs={{0,8},{1,2},{2,1},{3,4},{4,3},{5,6},{6,5},{7,15},{8,0},{9,10},{10,... | collective-permute-start | bytes 786440 | tf_op jit(solution)/shard_map/ppermute | solution.py:284
  14.9 0.0 collective-permute-done.5
  14.9 0.0 collective-permute-done.6.refs_6_
  14.9 3.6 %inner_rows.1.refs_7_ = f32[15,16,2,8,128]{4,3,2,1,0:T(8,128)S(1)} custom-call(s32[3]{0:T(128)S(1)} %pad_add_fusion.place_ref, f32[2,16,2048]{2,1,0:T(8,128)S(1)} %bitcast.7, f32[2,16,2048]{2,1,0:T(8,128)S(1)} %bitcast.10, f32[1,16,2048]{2,1,0:T(8,128)S(1)} %get-tuple-element.15.refs_0_.refs_2_, f32[1,16,2048]{2,1,0:T(8,128)S(1)} %collective-permute-done.refs_1_.refs_3_, ...), custom_call_target="tpu_custom_call" | custom-call | flops 11796480 | bytes 18874368 | tf_op jit(solution)/shard_map/inner_rows/pallas_call | solution.py:333
  18.5 3.3 %collective-permute-done.3 = f32[1,2,16,2048]{3,2,1,0:T(8,128)S(1)} collective-permute-done((f32[1,2,16,2048]{3,2,1,0:T(8,128)S(1)}, f32[1,2,16,2048]{3,2,1,0:T(8,128)S(1)}, u32[]{:S(2)}, u32[]{:S(2)}) %collective-permute-start.3) | collective-permute-done | bytes 262176 | tf_op jit(solution)/shard_map/ppermute | solution.py:284
  21.8 0.0 collective-permute-done.4.refs_6_
  21.8 3.6 %outer_rows.1 = f32[2,16,2048]{2,1,0:T(8,128)} custom-call(s32[3]{0:T(128)S(1)} %pad_add_fusion.place_ref, f32[2,16,2048]{2,1,0:T(8,128)S(1)} %bitcast.8, f32[2,16,2048]{2,1,0:T(8,128)S(1)} %bitcast.9, f32[1,16,2048]{2,1,0:T(8,128)S(1)} %get-tuple-element.15.refs_0_.refs_2_, f32[1,16,2048]{2,1,0:T(8,128)S(1)} %collective-permute-done.refs_1_.refs_3_, ...), custom_call_target="tpu_custom_call" | custom-call | tf_op jit(solution)/shard_map/outer_rows/pallas_call | solution.py:347
  (1 shorter events, 0.0 us)
Async XLA Ops:
  0.0 13.2 %copy-start = (f32[1,2,16,2048]{3,2,1,0:T(8,128)S(1)}, f32[1,2,16,2048]{3,2,1,0:T(8,128)}, u32[]{:S(2)}) copy-start(f32[1,2,16,2048]{3,2,1,0:T(8,128)} %field_ref.1) | copy-start | bytes 786436
  0.0 7.2 %collective-permute-start = (f32[1,16,2048]{2,1,0:T(8,128)}, f32[1,16,2048]{2,1,0:T(8,128)S(1)}, u32[]{:S(2)}, u32[]{:S(2)}) collective-permute-start(f32[1,16,2048]{2,1,0:T(8,128)} %medium_ref.1), channel_id=1, source_target_pairs={{0,8},{1,9},{2,10},{3,11},{4,12},{5,13},{6,14},{7,15},{8,0},{9,1},... | collective-permute-start | bytes 393224 | tf_op jit(solution)/shard_map/ppermute | solution.py:284
  2.9 8.0 %collective-permute-start.1 = (f32[1,16,2048]{2,1,0:T(8,128)}, f32[1,16,2048]{2,1,0:T(8,128)S(1)}, u32[]{:S(2)}, u32[]{:S(2)}) collective-permute-start(f32[1,16,2048]{2,1,0:T(8,128)} %medium_ref.1), channel_id=1, source_target_pairs={{0,16},{1,17},{2,18},{3,19},{4,20},{5,21},{6,22},{7,23},{8,24},{9,... | collective-permute-start | bytes 393224 | tf_op jit(solution)/shard_map/ppermute | solution.py:284
  4.5 6.5 %collective-permute-start.2 = (f32[1,16,2048]{2,1,0:T(8,128)}, f32[1,16,2048]{2,1,0:T(8,128)S(1)}, u32[]{:S(2)}, u32[]{:S(2)}) collective-permute-start(f32[1,16,2048]{2,1,0:T(8,128)} %medium_ref.1), channel_id=1, source_target_pairs={{0,24},{1,25},{2,26},{3,27},{4,28},{5,29},{6,30},{7,31},{8,16},{9,... | collective-permute-start | bytes 393224 | tf_op jit(solution)/shard_map/ppermute | solution.py:284
  11.0 3.9 %collective-permute-start.6 = (f32[4,16,2048]{2,1,0:T(8,128)S(1)}, f32[4,16,2048]{2,1,0:T(8,128)S(1)}, u32[]{:S(2)}, u32[]{:S(2)}) collective-permute-start(f32[4,16,2048]{2,1,0:T(8,128)S(1)} %pad_maximum_fusion), channel_id=1, source_target_pairs={{0,1},{1,0},{2,3},{3,2},{4,5},{5,4},{6,7},{7,6},{8,9},{9,8},{10,11... | collective-permute-start | bytes 1572872 | tf_op jit(solution)/shard_map/ppermute | solution.py:284
  11.9 10.0 %collective-permute-start.4 = (f32[16,40,128]{2,1,0:T(8,128)S(1)}, f32[16,40,128]{2,1,0:T(8,128)S(1)}, u32[]{:S(2)}, u32[]{:S(2)}) collective-permute-start(f32[16,40,128]{2,1,0:T(8,128)S(1)} %pack_rows.1), channel_id=1, source_target_pairs={{0,8},{1,2},{2,1},{3,4},{4,3},{5,6},{6,5},{7,15},{8,0},{9,10},{10,... | collective-permute-start | bytes 983048 | tf_op jit(solution)/shard_map/ppermute | solution.py:284
  13.2 1.7 %collective-permute-start.5 = (f32[1,2,16,2048]{3,2,1,0:T(8,128)S(1)}, f32[1,2,16,2048]{3,2,1,0:T(8,128)S(1)}, u32[]{:S(2)}, u32[]{:S(2)}) collective-permute-start(f32[1,2,16,2048]{3,2,1,0:T(8,128)S(1)} %copy-done), channel_id=1, source_target_pairs={{0,1},{1,0},{2,3},{3,2},{4,5},{5,4},{6,7},{7,6},{8,9},{9,8},{10,11... | collective-permute-start | bytes 786440 | tf_op jit(solution)/shard_map/ppermute | solution.py:284
  13.6 8.2 %collective-permute-start.3 = (f32[1,2,16,2048]{3,2,1,0:T(8,128)S(1)}, f32[1,2,16,2048]{3,2,1,0:T(8,128)S(1)}, u32[]{:S(2)}, u32[]{:S(2)}) collective-permute-start(f32[1,2,16,2048]{3,2,1,0:T(8,128)S(1)} %copy-done), channel_id=1, source_target_pairs={{0,8},{1,2},{2,1},{3,4},{4,3},{5,6},{6,5},{7,15},{8,0},{9,10},{10,... | collective-permute-start | bytes 786440 | tf_op jit(solution)/shard_map/ppermute | solution.py:284

commit v4 on v3

--- a/solution.py
+++ b/solution.py
@@ -19,6 +19,10 @@
 
 def sec_swap(sec, tiles, k):
     return [(s * tiles + t, (s ^ k) * tiles + t) for s in range(sec) for t in range(tiles)]
+
+
+def far_bits(k):
+    return k ^ (k >> 1)
 
 
 def pair_swap(sec, tiles):
@@ -82,13 +86,13 @@
     pl.when(odd == 0)(functools.partial(body, False))
 
 
-def inner_kernel(place_ref, *refs, sections, first, rows, cols, steps):
+def inner_kernel(*refs, sections, first, rows, cols, steps):
     own_b, pair_b = refs[:2]
     own_m = refs[2 : 2 + sections]
     pair_m = refs[2 + sections]
     edge_ref = refs[3 + sections]
     field_a, field_b, work_a, work_b, med = refs[4 + sections :]
-    sec, odd = place_ref[0], place_ref[1]
+    sec, odd = lax.axis_index("sec"), lax.axis_index("tile") % 2
     chunks = cols // LANES
     depth = STAGES * steps
     mid = SUBLANES + rows
@@ -104,7 +108,7 @@
                     field_a[j, part, pl.ds(mid + t, SUBLANES), :] = own_b[part, src, col]
                     field_a[j, part, pl.ds(pair_at + t, SUBLANES), :] = pair_b[part, src, col]
                 for k in range(sections):
-                    slot = sec ^ k
+                    slot = sec ^ far_bits(k)
                     med[slot, j, pl.ds(mid + t, SUBLANES), :] = to_medium_term(
                         own_m[k][0, src, col]
                     )
@@ -141,15 +145,16 @@
     by_side(odd, run)
 
 
-def outer_kernel(place_ref, *refs, sections, first, rows, cols, steps):
+def outer_kernel(*refs, tiles, sections, first, rows, cols, steps):
     own_b, rim_b = refs[:2]
     own_m = refs[2 : 2 + sections]
     rim_m, edge_ref, out_ref, levels, med, coef, result, sems = refs[2 + sections :]
-    sec, odd, edge = place_ref[0], place_ref[1], place_ref[2]
+    sec, tile = lax.axis_index("sec"), lax.axis_index("tile")
+    odd = tile % 2
     chunks = cols // LANES
     depth = STAGES * steps
     mid = SUBLANES + rows
-    is_edge = edge == 1
+    is_edge = (tile == 0) | (tile == tiles - 1)
     parts = sems.shape[0]
     per_part = chunks // parts
 
@@ -174,7 +179,7 @@
                 ]
             for k in range(sections):
                 for t in row_groups(rows):
-                    med[sec ^ k, j, pl.ds(mid + t, SUBLANES), :] = to_medium_term(
+                    med[sec ^ far_bits(k), j, pl.ds(mid + t, SUBLANES), :] = to_medium_term(
                         own_m[k][0, pl.ds(t, SUBLANES), col]
                     )
             at = 0
@@ -236,9 +241,9 @@
     return [STAGES * (steps - step) for step in range(steps)]
 
 
-def pack_kernel(place_ref, *refs, sections, first, rows, cols, steps):
+def pack_kernel(*refs, sections, first, rows, cols, steps):
     own_m, rim_out = refs[:sections], refs[sections]
-    sec, odd = place_ref[0], place_ref[1]
+    sec, odd = lax.axis_index("sec"), lax.axis_index("tile") % 2
     chunks = cols // LANES
 
     def pack(k, at, lo, hi):
@@ -256,7 +261,7 @@
     at = 0
     for step, count in enumerate(rim_rows(rows, steps)):
         for k in range(sections):
-            mine = (sec ^ k) == first + step
+            mine = (sec ^ far_bits(k)) == first + step
             pl.when(mine & (odd == 1))(pack(k, at, rows - count, rows))
             pl.when(mine & (odd == 0))(pack(k, at, 0, count))
         at += count
@@ -276,18 +281,12 @@
 def per_device(beams, medium):
     sections, tiles = lax.axis_size("sec"), lax.axis_size("tile")
     _, rows, cols = medium.shape
-    sec, tile = lax.axis_index("sec"), lax.axis_index("tile")
-    odd = tile % 2
-    place = jnp.stack(
-        [sec, odd, ((tile == 0) | (tile == tiles - 1)).astype(jnp.int32)]
-    ).astype(jnp.int32)
     swap = lambda value, pairs: lax.ppermute(value, AXES, pairs)
     pair, rim = pair_swap(sections, tiles), rim_swap(sections, tiles)
 
-    far = [swap(medium, sec_swap(sections, tiles, k)) for k in range(1, sections)]
+    far = [swap(medium, sec_swap(sections, tiles, far_bits(k))) for k in range(1, sections)]
     chunks = cols // LANES
     high = 2 * SUBLANES + 3 * rows
-    smem = pl.BlockSpec(memory_space=pltpu.SMEM)
     whole = pl.BlockSpec(memory_space=pltpu.VMEM)
     buffers = [pltpu.VMEM((chunks, 2, high, LANES), jnp.float32)] * 4 + [
         pltpu.VMEM((sections, chunks, high, LANES), jnp.float32)
@@ -310,22 +309,24 @@
     for first in range(0, sections, group):
         steps = min(group, sections - first)
         depth = STAGES * steps
-        sent = field if first > 0 else beams
-        pair_field, rim_field = swap(sent, pair), swap(sent, rim)
+        pair_field = swap(field if first > 0 else beams, pair)
+        rim_parts = [swap(field[:, part], rim) for part in range(2)]
         *own, field = lax.optimization_barrier((*own, field))
         fixed = dict(sections=sections, first=first, rows=rows, cols=cols, steps=steps)
-        pair_pack = jnp.concatenate(own, axis=0)
         rim_pack = pl.pallas_call(
             functools.partial(pack_kernel, **fixed),
             out_shape=jax.ShapeDtypeStruct(
                 (chunks, sum(rim_rows(rows, steps)), LANES), jnp.float32
             ),
-            in_specs=[smem] + [whole] * sections,
+            in_specs=[whole] * sections,
             out_specs=whole,
             compiler_params=params,
             name="pack_rows",
-        )(place, *own)
-        rim_pack, pair_pack = swap(rim_pack, rim), swap(pair_pack, pair)
+        )(*own)
+        *near, re, im, _ = lax.optimization_barrier((*own, *rim_parts, rim_pack))
+        rim_field = jnp.stack([re, im], axis=1)
+        rim_pack = swap(rim_pack, rim)
+        pair_pack = swap(jnp.concatenate(near, axis=0), pair)
         own_field, pair_field, rim_field = (
             value.reshape(2, rows, cols) for value in (field, pair_field, rim_field)
         )
@@ -335,7 +336,7 @@
             out_shape=jax.ShapeDtypeStruct(
                 (depth - 1, chunks, 2, SUBLANES, LANES), jnp.float32
             ),
-            in_specs=[smem] + [whole] * (3 + sections),
+            in_specs=[whole] * (3 + sections),
             out_specs=whole,
             scratch_shapes=buffers,
             compiler_params=params,
@@ -343,11 +344,11 @@
                 flops=10 * work, bytes_accessed=16 * work, transcendentals=0
             ),
             name="inner_rows",
-        )(place, own_field, pair_field, *own, pair_pack)
+        )(own_field, pair_field, *own, pair_pack)
         field = pl.pallas_call(
-            functools.partial(outer_kernel, **fixed),
+            functools.partial(outer_kernel, tiles=tiles, **fixed),
             out_shape=jax.ShapeDtypeStruct((2, rows, cols), jnp.float32),
-            in_specs=[smem] + [whole] * (4 + sections),
+            in_specs=[whole] * (4 + sections),
             out_specs=pl.BlockSpec(memory_space=pl.ANY),
             scratch_shapes=[
                 pltpu.VMEM((depth, chunks, 2, high, LANES), jnp.float32),
@@ -358,7 +359,7 @@
             ],
             compiler_params=params,
             name="outer_rows",
-        )(place, own_field, rim_field, *own, rim_pack, edges)[None]
+        )(own_field, rim_field, *own, rim_pack, edges)[None]
     return field
 
 

time: 25.6 us -> 22.9 us (0.89)
  Pallas kernels: 9.02 us -> 7.24 us
  waiting for transfers between devices: 8.76 us -> 7.16 us
  starting transfers between devices: 7.51 us -> 8.23 us
    ppermute x7 -> x8, waiting for transfers between devices: 8.76 us -> 7.16 us  [per_device(): swap = lambda value, pairs: lax.ppermute(value, AXES, pairs)]
    ppermute x7 -> x8, starting transfers between devices: 7.51 us -> 8.23 us  [per_device(): swap = lambda value, pairs: lax.ppermute(value, AXES, pairs)]
    pallas_call x1, Pallas kernels: 3.65 us -> 2.99 us  [per_device(): pl.pallas_call(functools.partial(outer_kernel, tiles=tiles, **fixed), out...]
    pallas_call x1, Pallas kernels: 3.63 us -> 3.06 us  [per_device(): pl.pallas_call(functools.partial(inner_kernel, **fixed), out_shape=jax.Sh...]
    pallas_call x1, Pallas kernels: 0.72 us -> 0.17 us  [per_device(): pl.pallas_call(functools.partial(pack_kernel, **fixed), out_shape=jax.Sha...]
  transfers between devices with their start and end apart: 7 -> 8, of which waited for: 3 -> 4; matrix products, arithmetic and copies ran while one was open for 0% -> 0% of each run, Pallas kernels for 21% -> 19%
where the time goes in v4:
time: 22.9 us; the launch traced here: 22.8 us
  starting transfers between devices  8.23 us (36%)
  Pallas kernels  7.24 us (32%)
  waiting for transfers between devices  7.16 us (31%)
    ppermute x8, starting transfers between devices, per_device(): swap = lambda value, pairs: lax.ppermute(value, AXES, pairs)  8.23 us
    ppermute x8, waiting for transfers between devices, per_device(): swap = lambda value, pairs: lax.ppermute(value, AXES, pairs)  7.16 us
    pallas_call x1, Pallas kernels, per_device(): pl.pallas_call(functools.partial(inner_kernel, **fixed), out_shape=jax.Sh...  3.06 us
    pallas_call x1, Pallas kernels, per_device(): pl.pallas_call(functools.partial(outer_kernel, tiles=tiles, **fixed), out...  2.99 us
    pallas_call x1, Pallas kernels, per_device(): pl.pallas_call(load_kernel, out_shape=(pltpu.VMEM(beams.shape, beams.dtyp...  1.03 us
  transfers between devices with their start and end apart: 8, of which 4 were waited for; matrix products, arithmetic and copies ran while one was open for 0% of the time, Pallas kernels for 19%

profile of v4, /device:TPU:0, one launch (start us, length us, event | category | flops | bytes accessed | tf_op | source)
XLA Modules:
  0.0 22.8 jit_solution(15605159576275966479)
XLA Ops:
  0.0 0.0 copy-start
  0.0 2.9 %collective-permute-start = (f32[1,16,2048]{2,1,0:T(8,128)}, f32[1,16,2048]{2,1,0:T(8,128)S(1)}, u32[]{:S(2)}, u32[]{:S(2)}) collective-permute-start(f32[1,16,2048]{2,1,0:T(8,128)} %medium_ref.1), channel_id=1, source_target_pairs={{0,8},{1,9},{2,10},{3,11},{4,12},{5,13},{6,14},{7,15},{8,0},{9,1},... | collective-permute-start | bytes 393224 | tf_op jit(solution)/shard_map/ppermute | solution.py:284
  2.9 1.5 %collective-permute-start.2 = (f32[1,16,2048]{2,1,0:T(8,128)}, f32[1,16,2048]{2,1,0:T(8,128)S(1)}, u32[]{:S(2)}, u32[]{:S(2)}) collective-permute-start(f32[1,16,2048]{2,1,0:T(8,128)} %medium_ref.1), channel_id=1, source_target_pairs={{0,16},{1,17},{2,18},{3,19},{4,20},{5,21},{6,22},{7,23},{8,24},{9,... | collective-permute-start | bytes 393224 | tf_op jit(solution)/shard_map/ppermute | solution.py:284
  4.5 0.0 collective-permute-start.1
  4.5 1.0 %load_arguments.1 = (f32[1,2,16,2048]{3,2,1,0:T(8,128)S(1)}, f32[1,16,2048]{2,1,0:T(8,128)S(1)}) custom-call(f32[1,2,16,2048]{3,2,1,0:T(8,128)} %field_ref.1, f32[1,16,2048]{2,1,0:T(8,128)} %medium_ref.1), custom_call_target="tpu_custom_call" | custom-call | bytes 2097152 | tf_op jit(solution)/shard_map/load_arguments/pallas_call | solution.py:295
  5.5 2.0 %collective-permute-start.4 = (f32[1,16,2048]{2,1,0:T(8,128)S(1)}, f32[1,16,2048]{2,1,0:T(8,128)S(1)}, u32[]{:S(2)}, u32[]{:S(2)}) collective-permute-start(f32[1,16,2048]{2,1,0:T(8,128)S(1)} %get-tuple-element.31), channel_id=1, source_target_pairs={{0,8},{1,2},{2,1},{3,4},{4,3},{5,6},{6,5},{7,15},{8,0},{9,10},{10,... | collective-permute-start | bytes 393224 | tf_op jit(solution)/shard_map/ppermute | solution.py:284
  7.6 0.1 collective-permute-start.3
  7.6 0.0 collective-permute-done.refs_1_.refs_3_
  7.6 3.3 %collective-permute-done.2.refs_3_.refs_5_ = f32[1,16,2048]{2,1,0:T(8,128)S(1)} collective-permute-done((f32[1,16,2048]{2,1,0:T(8,128)}, f32[1,16,2048]{2,1,0:T(8,128)S(1)}, u32[]{:S(2)}, u32[]{:S(2)}) %collective-permute-start.2) | collective-permute-done | bytes 131104 | tf_op jit(solution)/shard_map/ppermute | solution.py:284
  10.9 0.0 collective-permute-done.1.refs_2_.refs_4_
  10.9 0.2 pack_rows.1
  11.1 0.0 collective-permute-done.4
  11.1 1.4 %collective-permute-done.3 = f32[1,16,2048]{2,1,0:T(8,128)S(1)} collective-permute-done((f32[1,16,2048]{2,1,0:T(8,128)S(1)}, f32[1,16,2048]{2,1,0:T(8,128)S(1)}, u32[]{:S(2)}, u32[]{:S(2)}) %collective-permute-start.3) | collective-permute-done | bytes 131104 | tf_op jit(solution)/shard_map/ppermute | solution.py:284
  12.6 0.1 collective-permute-start.7
  12.6 1.6 %collective-permute-start.5 = (f32[16,40,128]{2,1,0:T(8,128)S(1)}, f32[16,40,128]{2,1,0:T(8,128)S(1)}, u32[]{:S(2)}, u32[]{:S(2)}) collective-permute-start(f32[16,40,128]{2,1,0:T(8,128)S(1)} %pack_rows.1), channel_id=1, source_target_pairs={{0,8},{1,2},{2,1},{3,4},{4,3},{5,6},{6,5},{7,15},{8,0},{9,10},{10,... | collective-permute-start | bytes 983048 | tf_op jit(solution)/shard_map/ppermute | solution.py:284
  14.2 0.0 copy-done
  14.2 0.0 collective-permute-start.6
  14.3 1.5 %collective-permute-done.6 = f32[1,2,16,2048]{3,2,1,0:T(8,128)S(1)} collective-permute-done((f32[1,2,16,2048]{3,2,1,0:T(8,128)S(1)}, f32[1,2,16,2048]{3,2,1,0:T(8,128)S(1)}, u32[]{:S(2)}, u32[]{:S(2)}) %collective-permute-start.6) | collective-permute-done | bytes 262176 | tf_op jit(solution)/shard_map/ppermute | solution.py:284
  15.8 0.0 collective-permute-done.7.refs_6_
  15.8 3.1 %inner_rows.1.refs_7_ = f32[15,16,2,8,128]{4,3,2,1,0:T(8,128)S(1)} custom-call(f32[2,16,2048]{2,1,0:T(8,128)S(1)} %bitcast.11, f32[2,16,2048]{2,1,0:T(8,128)S(1)} %bitcast.13, f32[1,16,2048]{2,1,0:T(8,128)S(1)} %get-tuple-element.27.refs_0_.refs_2_, f32[1,16,2048]{2,1,0:T(8,128)S(1)} %collective-permute-done.refs_1_.refs_3_, ...), custom_call_target="tpu_custom_call" | custom-call | flops 11796480 | bytes 18874368 | tf_op jit(solution)/shard_map/inner_rows/pallas_call | solution.py:334
  18.8 0.9 %collective-permute-done.5.refs_6_ = f32[16,40,128]{2,1,0:T(8,128)S(1)} collective-permute-done((f32[16,40,128]{2,1,0:T(8,128)S(1)}, f32[16,40,128]{2,1,0:T(8,128)S(1)}, u32[]{:S(2)}, u32[]{:S(2)}) %collective-permute-start.5) | collective-permute-done | bytes 327712 | tf_op jit(solution)/shard_map/ppermute | solution.py:284
  19.8 3.0 %outer_rows.1 = f32[2,16,2048]{2,1,0:T(8,128)} custom-call(f32[2,16,2048]{2,1,0:T(8,128)S(1)} %bitcast.12, f32[2,16,2048]{2,1,0:T(8,128)S(1)} %maximum_bitcast_fusion.refs_1_, f32[1,16,2048]{2,1,0:T(8,128)S(1)} %get-tuple-element.27.refs_0_.refs_2_, f32[1,16,2048]{2,1,0:T(8,128)S(1)} %collective-permute-done.refs_1_.refs_3_, ...), custom_call_target="tpu_custom_call" | custom-call | tf_op jit(solution)/shard_map/outer_rows/pallas_call | solution.py:348
  (3 shorter events, 0.1 us)
Async XLA Ops:
  0.0 14.2 %copy-start = (f32[1,2,16,2048]{3,2,1,0:T(8,128)S(1)}, f32[1,2,16,2048]{3,2,1,0:T(8,128)}, u32[]{:S(2)}) copy-start(f32[1,2,16,2048]{3,2,1,0:T(8,128)} %field_ref.1) | copy-start | bytes 786436
  0.0 7.6 %collective-permute-start = (f32[1,16,2048]{2,1,0:T(8,128)}, f32[1,16,2048]{2,1,0:T(8,128)S(1)}, u32[]{:S(2)}, u32[]{:S(2)}) collective-permute-start(f32[1,16,2048]{2,1,0:T(8,128)} %medium_ref.1), channel_id=1, source_target_pairs={{0,8},{1,9},{2,10},{3,11},{4,12},{5,13},{6,14},{7,15},{8,0},{9,1},... | collective-permute-start | bytes 393224 | tf_op jit(solution)/shard_map/ppermute | solution.py:284
  2.9 8.0 %collective-permute-start.2 = (f32[1,16,2048]{2,1,0:T(8,128)}, f32[1,16,2048]{2,1,0:T(8,128)S(1)}, u32[]{:S(2)}, u32[]{:S(2)}) collective-permute-start(f32[1,16,2048]{2,1,0:T(8,128)} %medium_ref.1), channel_id=1, source_target_pairs={{0,16},{1,17},{2,18},{3,19},{4,20},{5,21},{6,22},{7,23},{8,24},{9,... | collective-permute-start | bytes 393224 | tf_op jit(solution)/shard_map/ppermute | solution.py:284
  4.5 6.5 %collective-permute-start.1 = (f32[1,16,2048]{2,1,0:T(8,128)}, f32[1,16,2048]{2,1,0:T(8,128)S(1)}, u32[]{:S(2)}, u32[]{:S(2)}) collective-permute-start(f32[1,16,2048]{2,1,0:T(8,128)} %medium_ref.1), channel_id=1, source_target_pairs={{0,24},{1,25},{2,26},{3,27},{4,28},{5,29},{6,30},{7,31},{8,16},{9,... | collective-permute-start | bytes 393224 | tf_op jit(solution)/shard_map/ppermute | solution.py:284
  5.5 5.6 %collective-permute-start.4 = (f32[1,16,2048]{2,1,0:T(8,128)S(1)}, f32[1,16,2048]{2,1,0:T(8,128)S(1)}, u32[]{:S(2)}, u32[]{:S(2)}) collective-permute-start(f32[1,16,2048]{2,1,0:T(8,128)S(1)} %get-tuple-element.31), channel_id=1, source_target_pairs={{0,8},{1,2},{2,1},{3,4},{4,3},{5,6},{6,5},{7,15},{8,0},{9,10},{10,... | collective-permute-start | bytes 393224 | tf_op jit(solution)/shard_map/ppermute | solution.py:284
  7.6 5.0 %collective-permute-start.3 = (f32[1,16,2048]{2,1,0:T(8,128)S(1)}, f32[1,16,2048]{2,1,0:T(8,128)S(1)}, u32[]{:S(2)}, u32[]{:S(2)}) collective-permute-start(f32[1,16,2048]{2,1,0:T(8,128)S(1)} %get-tuple-element.32), channel_id=1, source_target_pairs={{0,8},{1,2},{2,1},{3,4},{4,3},{5,6},{6,5},{7,15},{8,0},{9,10},{10,... | collective-permute-start | bytes 393224 | tf_op jit(solution)/shard_map/ppermute | solution.py:284
  12.6 3.2 %collective-permute-start.7 = (f32[4,16,2048]{2,1,0:T(8,128)S(1)}, f32[4,16,2048]{2,1,0:T(8,128)S(1)}, u32[]{:S(2)}, u32[]{:S(2)}) collective-permute-start(f32[4,16,2048]{2,1,0:T(8,128)S(1)} %pad_maximum_fusion), channel_id=1, source_target_pairs={{0,1},{1,0},{2,3},{3,2},{4,5},{5,4},{6,7},{7,6},{8,9},{9,8},{10,11... | collective-permute-start | bytes 1572872 | tf_op jit(solution)/shard_map/ppermute | solution.py:284
  12.6 7.1 %collective-permute-start.5 = (f32[16,40,128]{2,1,0:T(8,128)S(1)}, f32[16,40,128]{2,1,0:T(8,128)S(1)}, u32[]{:S(2)}, u32[]{:S(2)}) collective-permute-start(f32[16,40,128]{2,1,0:T(8,128)S(1)} %pack_rows.1), channel_id=1, source_target_pairs={{0,8},{1,2},{2,1},{3,4},{4,3},{5,6},{6,5},{7,15},{8,0},{9,10},{10,... | collective-permute-start | bytes 983048 | tf_op jit(solution)/shard_map/ppermute | solution.py:284
  14.2 1.5 %collective-permute-start.6 = (f32[1,2,16,2048]{3,2,1,0:T(8,128)S(1)}, f32[1,2,16,2048]{3,2,1,0:T(8,128)S(1)}, u32[]{:S(2)}, u32[]{:S(2)}) collective-permute-start(f32[1,2,16,2048]{3,2,1,0:T(8,128)S(1)} %copy-done), channel_id=1, source_target_pairs={{0,1},{1,0},{2,3},{3,2},{4,5},{5,4},{6,7},{7,6},{8,9},{9,8},{10,11... | collective-permute-start | bytes 786440 | tf_op jit(solution)/shard_map/ppermute | solution.py:284

commit v5 on v4

--- a/solution.py
+++ b/solution.py
@@ -89,9 +89,9 @@
 def inner_kernel(*refs, sections, first, rows, cols, steps):
     own_b, pair_b = refs[:2]
     own_m = refs[2 : 2 + sections]
-    pair_m = refs[2 + sections]
-    edge_ref = refs[3 + sections]
-    field_a, field_b, work_a, work_b, med = refs[4 + sections :]
+    pair_m = refs[2 + sections : 2 + 2 * sections]
+    edge_ref = refs[2 + 2 * sections]
+    field_a, field_b, work_a, work_b, med = refs[3 + 2 * sections :]
     sec, odd = lax.axis_index("sec"), lax.axis_index("tile") % 2
     chunks = cols // LANES
     depth = STAGES * steps
@@ -113,7 +113,7 @@
                         own_m[k][0, src, col]
                     )
                     med[slot, j, pl.ds(pair_at + t, SUBLANES), :] = to_medium_term(
-                        pair_m[k, src, col]
+                        pair_m[k][0, src, col]
                     )
         begin, end = field_a, field_b
         level = 0
@@ -326,7 +326,7 @@
         *near, re, im, _ = lax.optimization_barrier((*own, *rim_parts, rim_pack))
         rim_field = jnp.stack([re, im], axis=1)
         rim_pack = swap(rim_pack, rim)
-        pair_pack = swap(jnp.concatenate(near, axis=0), pair)
+        pair_m = [swap(piece, pair) for piece in near]
         own_field, pair_field, rim_field = (
             value.reshape(2, rows, cols) for value in (field, pair_field, rim_field)
         )
@@ -336,7 +336,7 @@
             out_shape=jax.ShapeDtypeStruct(
                 (depth - 1, chunks, 2, SUBLANES, LANES), jnp.float32
             ),
-            in_specs=[whole] * (3 + sections),
+            in_specs=[whole] * (2 + 2 * sections),
             out_specs=whole,
             scratch_shapes=buffers,
             compiler_params=params,
@@ -344,7 +344,7 @@
                 flops=10 * work, bytes_accessed=16 * work, transcendentals=0
             ),
             name="inner_rows",
-        )(own_field, pair_field, *own, pair_pack)
+        )(own_field, pair_field, *own, *pair_m)
         field = pl.pallas_call(
             functools.partial(outer_kernel, tiles=tiles, **fixed),
             out_shape=jax.ShapeDtypeStruct((2, rows, cols), jnp.float32),

time: 22.9 us -> 21.4 us (0.934)
  waiting for transfers between devices: 7.16 us -> 3.15 us
  starting transfers between devices: 8.23 us -> 10.8 us
    ppermute x8 -> x11, waiting for transfers between devices: 7.16 us -> 3.15 us  [per_device(): swap = lambda value, pairs: lax.ppermute(value, AXES, pairs)]
    ppermute x8 -> x11, starting transfers between devices: 8.23 us -> 10.8 us  [per_device(): swap = lambda value, pairs: lax.ppermute(value, AXES, pairs)]
  transfers between devices with their start and end apart: 8 -> 11, of which waited for: 4 -> 7; matrix products, arithmetic and copies ran while one was open for 0% -> 0% of each run, Pallas kernels for 19% -> 20%
where the time goes in v5:
time: 21.4 us; the launch traced here: 21.2 us
  starting transfers between devices  10.8 us (50%)
  Pallas kernels  7.24 us (34%)
  waiting for transfers between devices  3.15 us (15%)
    ppermute x11, starting transfers between devices, per_device(): swap = lambda value, pairs: lax.ppermute(value, AXES, pairs)  10.8 us
    ppermute x11, waiting for transfers between devices, per_device(): swap = lambda value, pairs: lax.ppermute(value, AXES, pairs)  3.15 us
    pallas_call x1, Pallas kernels, per_device(): pl.pallas_call(functools.partial(inner_kernel, **fixed), out_shape=jax.Sh...  3.06 us
    pallas_call x1, Pallas kernels, per_device(): pl.pallas_call(functools.partial(outer_kernel, tiles=tiles, **fixed), out...  2.99 us
    pallas_call x1, Pallas kernels, per_device(): pl.pallas_call(load_kernel, out_shape=(pltpu.VMEM(beams.shape, beams.dtyp...  1.03 us
  transfers between devices with their start and end apart: 11, of which 7 were waited for; matrix products, arithmetic and copies ran while one was open for 0% of the time, Pallas kernels for 20%

profile of v5, /device:TPU:0, one launch (start us, length us, event | category | flops | bytes accessed | tf_op | source)
XLA Modules:
  0.0 21.2 jit_solution(14688258467400859401)
XLA Ops:
  0.0 2.9 %collective-permute-start = (f32[1,16,2048]{2,1,0:T(8,128)}, f32[1,16,2048]{2,1,0:T(8,128)S(1)}, u32[]{:S(2)}, u32[]{:S(2)}) collective-permute-start(f32[1,16,2048]{2,1,0:T(8,128)} %medium_ref.1), channel_id=1, source_target_pairs={{0,8},{1,9},{2,10},{3,11},{4,12},{5,13},{6,14},{7,15},{8,0},{9,1},... | collective-permute-start | bytes 393224 | tf_op jit(solution)/shard_map/ppermute | solution.py:284
  2.9 1.5 %collective-permute-start.2 = (f32[1,16,2048]{2,1,0:T(8,128)}, f32[1,16,2048]{2,1,0:T(8,128)S(1)}, u32[]{:S(2)}, u32[]{:S(2)}) collective-permute-start(f32[1,16,2048]{2,1,0:T(8,128)} %medium_ref.1), channel_id=1, source_target_pairs={{0,16},{1,17},{2,18},{3,19},{4,20},{5,21},{6,22},{7,23},{8,24},{9,... | collective-permute-start | bytes 393224 | tf_op jit(solution)/shard_map/ppermute | solution.py:284
  4.5 0.0 collective-permute-start.1
  4.5 0.0 collective-permute-start.6
  4.5 1.0 %load_arguments.1 = (f32[1,2,16,2048]{3,2,1,0:T(8,128)S(1)}, f32[1,16,2048]{2,1,0:T(8,128)S(1)}) custom-call(f32[1,2,16,2048]{3,2,1,0:T(8,128)} %field_ref.1, f32[1,16,2048]{2,1,0:T(8,128)} %medium_ref.1), custom_call_target="tpu_custom_call" | custom-call | bytes 2097152 | tf_op jit(solution)/shard_map/load_arguments/pallas_call | solution.py:295
  5.5 2.0 %collective-permute-start.4 = (f32[1,16,2048]{2,1,0:T(8,128)S(1)}, f32[1,16,2048]{2,1,0:T(8,128)S(1)}, u32[]{:S(2)}, u32[]{:S(2)}) collective-permute-start(f32[1,16,2048]{2,1,0:T(8,128)S(1)} %get-tuple-element.31), channel_id=1, source_target_pairs={{0,8},{1,2},{2,1},{3,4},{4,3},{5,6},{6,5},{7,15},{8,0},{9,10},{10,... | collective-permute-start | bytes 393224 | tf_op jit(solution)/shard_map/ppermute | solution.py:284
  7.6 0.0 collective-permute-done.refs_1_.refs_3_
  7.6 2.0 %collective-permute-start.3 = (f32[1,16,2048]{2,1,0:T(8,128)S(1)}, f32[1,16,2048]{2,1,0:T(8,128)S(1)}, u32[]{:S(2)}, u32[]{:S(2)}) collective-permute-start(f32[1,16,2048]{2,1,0:T(8,128)S(1)} %get-tuple-element.32), channel_id=1, source_target_pairs={{0,8},{1,2},{2,1},{3,4},{4,3},{5,6},{6,5},{7,15},{8,0},{9,10},{10,... | collective-permute-start | bytes 393224 | tf_op jit(solution)/shard_map/ppermute | solution.py:284
  9.5 1.4 %collective-permute-done.2.refs_3_.refs_5_ = f32[1,16,2048]{2,1,0:T(8,128)S(1)} collective-permute-done((f32[1,16,2048]{2,1,0:T(8,128)}, f32[1,16,2048]{2,1,0:T(8,128)S(1)}, u32[]{:S(2)}, u32[]{:S(2)}) %collective-permute-start.2) | collective-permute-done | bytes 131104 | tf_op jit(solution)/shard_map/ppermute | solution.py:284
  10.9 0.0 collective-permute-done.1.refs_2_.refs_4_
  10.9 0.2 pack_rows.1
  11.1 1.3 %collective-permute-start.5 = (f32[16,40,128]{2,1,0:T(8,128)S(1)}, f32[16,40,128]{2,1,0:T(8,128)S(1)}, u32[]{:S(2)}, u32[]{:S(2)}) collective-permute-start(f32[16,40,128]{2,1,0:T(8,128)S(1)} %pack_rows.1), channel_id=1, source_target_pairs={{0,8},{1,2},{2,1},{3,4},{4,3},{5,6},{6,5},{7,15},{8,0},{9,10},{10,... | collective-permute-start | bytes 983048 | tf_op jit(solution)/shard_map/ppermute | solution.py:284
  12.4 0.0 collective-permute-done.4
  12.4 0.1 collective-permute-done.3
  12.5 0.3 %collective-permute-start.7 = (f32[1,16,2048]{2,1,0:T(8,128)S(1)}, f32[1,16,2048]{2,1,0:T(8,128)S(1)}, u32[]{:S(2)}, u32[]{:S(2)}) collective-permute-start(f32[1,16,2048]{2,1,0:T(8,128)S(1)} %get-tuple-element.27.refs_0_.refs_2_), channel_id=1, source_target_pairs={{0,1},{1,0},{2,3},{3,2},{4,5},{5,4},{6,7},{7,6},{8,9},{9,8},{10,11... | collective-permute-start | bytes 393224 | tf_op jit(solution)/shard_map/ppermute | solution.py:284
  12.9 0.2 collective-permute-start.8
  13.0 0.3 %collective-permute-start.9 = (f32[1,16,2048]{2,1,0:T(8,128)S(1)}, f32[1,16,2048]{2,1,0:T(8,128)S(1)}, u32[]{:S(2)}, u32[]{:S(2)}) collective-permute-start(f32[1,16,2048]{2,1,0:T(8,128)S(1)} %collective-permute-done.1.refs_2_.refs_4_), channel_id=1, source_target_pairs={{0,1},{1,0},{2,3},{3,2},{4,5},{5,4},{6,7},{7,6},{8,9},{9,8},{10,11... | collective-permute-start | bytes 393224 | tf_op jit(solution)/shard_map/ppermute | solution.py:284
  13.4 0.0 collective-permute-done.6
  13.4 0.2 collective-permute-start.10
  13.6 0.3 %collective-permute-done.7.refs_6_ = f32[1,16,2048]{2,1,0:T(8,128)S(1)} collective-permute-done((f32[1,16,2048]{2,1,0:T(8,128)S(1)}, f32[1,16,2048]{2,1,0:T(8,128)S(1)}, u32[]{:S(2)}, u32[]{:S(2)}) %collective-permute-start.7) | collective-permute-done | bytes 131104 | tf_op jit(solution)/shard_map/ppermute | solution.py:284
  13.9 0.3 %collective-permute-done.8.refs_7_ = f32[1,16,2048]{2,1,0:T(8,128)S(1)} collective-permute-done((f32[1,16,2048]{2,1,0:T(8,128)S(1)}, f32[1,16,2048]{2,1,0:T(8,128)S(1)}, u32[]{:S(2)}, u32[]{:S(2)}) %collective-permute-start.8) | collective-permute-done | bytes 131104 | tf_op jit(solution)/shard_map/ppermute | solution.py:284
  14.2 0.2 collective-permute-done.9.refs_8_
  14.4 0.3 %collective-permute-done.10.refs_9_ = f32[1,16,2048]{2,1,0:T(8,128)S(1)} collective-permute-done((f32[1,16,2048]{2,1,0:T(8,128)S(1)}, f32[1,16,2048]{2,1,0:T(8,128)S(1)}, u32[]{:S(2)}, u32[]{:S(2)}) %collective-permute-start.10) | collective-permute-done | bytes 131104 | tf_op jit(solution)/shard_map/ppermute | solution.py:284
  14.7 3.1 %inner_rows.1.refs_7_ = f32[15,16,2,8,128]{4,3,2,1,0:T(8,128)S(1)} custom-call(f32[2,16,2048]{2,1,0:T(8,128)S(1)} %bitcast.11, f32[2,16,2048]{2,1,0:T(8,128)S(1)} %bitcast.13, f32[1,16,2048]{2,1,0:T(8,128)S(1)} %get-tuple-element.27.refs_0_.refs_2_, f32[1,16,2048]{2,1,0:T(8,128)S(1)} %collective-permute-done.refs_1_.refs_3_, ...), custom_call_target="tpu_custom_call" | custom-call | flops 11796480 | bytes 18874368 | tf_op jit(solution)/shard_map/inner_rows/pallas_call | solution.py:334
  17.8 0.4 %collective-permute-done.5.refs_6_ = f32[16,40,128]{2,1,0:T(8,128)S(1)} collective-permute-done((f32[16,40,128]{2,1,0:T(8,128)S(1)}, f32[16,40,128]{2,1,0:T(8,128)S(1)}, u32[]{:S(2)}, u32[]{:S(2)}) %collective-permute-start.5) | collective-permute-done | bytes 327712 | tf_op jit(solution)/shard_map/ppermute | solution.py:284
  18.2 3.0 %outer_rows.1 = f32[2,16,2048]{2,1,0:T(8,128)} custom-call(f32[2,16,2048]{2,1,0:T(8,128)S(1)} %bitcast.12, f32[2,16,2048]{2,1,0:T(8,128)S(1)} %maximum_bitcast_fusion.refs_1_, f32[1,16,2048]{2,1,0:T(8,128)S(1)} %get-tuple-element.27.refs_0_.refs_2_, f32[1,16,2048]{2,1,0:T(8,128)S(1)} %collective-permute-done.refs_1_.refs_3_, ...), custom_call_target="tpu_custom_call" | custom-call | tf_op jit(solution)/shard_map/outer_rows/pallas_call | solution.py:348
  (2 shorter events, 0.0 us)
Async XLA Ops:
  0.0 7.6 %collective-permute-start = (f32[1,16,2048]{2,1,0:T(8,128)}, f32[1,16,2048]{2,1,0:T(8,128)S(1)}, u32[]{:S(2)}, u32[]{:S(2)}) collective-permute-start(f32[1,16,2048]{2,1,0:T(8,128)} %medium_ref.1), channel_id=1, source_target_pairs={{0,8},{1,9},{2,10},{3,11},{4,12},{5,13},{6,14},{7,15},{8,0},{9,1},... | collective-permute-start | bytes 393224 | tf_op jit(solution)/shard_map/ppermute | solution.py:284
  2.9 8.0 %collective-permute-start.2 = (f32[1,16,2048]{2,1,0:T(8,128)}, f32[1,16,2048]{2,1,0:T(8,128)S(1)}, u32[]{:S(2)}, u32[]{:S(2)}) collective-permute-start(f32[1,16,2048]{2,1,0:T(8,128)} %medium_ref.1), channel_id=1, source_target_pairs={{0,16},{1,17},{2,18},{3,19},{4,20},{5,21},{6,22},{7,23},{8,24},{9,... | collective-permute-start | bytes 393224 | tf_op jit(solution)/shard_map/ppermute | solution.py:284
  4.5 6.5 %collective-permute-start.1 = (f32[1,16,2048]{2,1,0:T(8,128)}, f32[1,16,2048]{2,1,0:T(8,128)S(1)}, u32[]{:S(2)}, u32[]{:S(2)}) collective-permute-start(f32[1,16,2048]{2,1,0:T(8,128)} %medium_ref.1), channel_id=1, source_target_pairs={{0,24},{1,25},{2,26},{3,27},{4,28},{5,29},{6,30},{7,31},{8,16},{9,... | collective-permute-start | bytes 393224 | tf_op jit(solution)/shard_map/ppermute | solution.py:284
  4.5 8.9 %collective-permute-start.6 = (f32[1,2,16,2048]{3,2,1,0:T(8,128)}, f32[1,2,16,2048]{3,2,1,0:T(8,128)S(1)}, u32[]{:S(2)}, u32[]{:S(2)}) collective-permute-start(f32[1,2,16,2048]{3,2,1,0:T(8,128)} %field_ref.1), channel_id=1, source_target_pairs={{0,1},{1,0},{2,3},{3,2},{4,5},{5,4},{6,7},{7,6},{8,9},{9,8},{10,11... | collective-permute-start | bytes 786440 | tf_op jit(solution)/shard_map/ppermute | solution.py:284
  5.5 6.9 %collective-permute-start.4 = (f32[1,16,2048]{2,1,0:T(8,128)S(1)}, f32[1,16,2048]{2,1,0:T(8,128)S(1)}, u32[]{:S(2)}, u32[]{:S(2)}) collective-permute-start(f32[1,16,2048]{2,1,0:T(8,128)S(1)} %get-tuple-element.31), channel_id=1, source_target_pairs={{0,8},{1,2},{2,1},{3,4},{4,3},{5,6},{6,5},{7,15},{8,0},{9,10},{10,... | collective-permute-start | bytes 393224 | tf_op jit(solution)/shard_map/ppermute | solution.py:284
  7.6 5.0 %collective-permute-start.3 = (f32[1,16,2048]{2,1,0:T(8,128)S(1)}, f32[1,16,2048]{2,1,0:T(8,128)S(1)}, u32[]{:S(2)}, u32[]{:S(2)}) collective-permute-start(f32[1,16,2048]{2,1,0:T(8,128)S(1)} %get-tuple-element.32), channel_id=1, source_target_pairs={{0,8},{1,2},{2,1},{3,4},{4,3},{5,6},{6,5},{7,15},{8,0},{9,10},{10,... | collective-permute-start | bytes 393224 | tf_op jit(solution)/shard_map/ppermute | solution.py:284
  11.1 7.1 %collective-permute-start.5 = (f32[16,40,128]{2,1,0:T(8,128)S(1)}, f32[16,40,128]{2,1,0:T(8,128)S(1)}, u32[]{:S(2)}, u32[]{:S(2)}) collective-permute-start(f32[16,40,128]{2,1,0:T(8,128)S(1)} %pack_rows.1), channel_id=1, source_target_pairs={{0,8},{1,2},{2,1},{3,4},{4,3},{5,6},{6,5},{7,15},{8,0},{9,10},{10,... | collective-permute-start | bytes 983048 | tf_op jit(solution)/shard_map/ppermute | solution.py:284
  12.5 1.3 %collective-permute-start.7 = (f32[1,16,2048]{2,1,0:T(8,128)S(1)}, f32[1,16,2048]{2,1,0:T(8,128)S(1)}, u32[]{:S(2)}, u32[]{:S(2)}) collective-permute-start(f32[1,16,2048]{2,1,0:T(8,128)S(1)} %get-tuple-element.27.refs_0_.refs_2_), channel_id=1, source_target_pairs={{0,1},{1,0},{2,3},{3,2},{4,5},{5,4},{6,7},{7,6},{8,9},{9,8},{10,11... | collective-permute-start | bytes 393224 | tf_op jit(solution)/shard_map/ppermute | solution.py:284
  12.9 1.3 %collective-permute-start.8 = (f32[1,16,2048]{2,1,0:T(8,128)S(1)}, f32[1,16,2048]{2,1,0:T(8,128)S(1)}, u32[]{:S(2)}, u32[]{:S(2)}) collective-permute-start(f32[1,16,2048]{2,1,0:T(8,128)S(1)} %collective-permute-done.refs_1_.refs_3_), channel_id=1, source_target_pairs={{0,1},{1,0},{2,3},{3,2},{4,5},{5,4},{6,7},{7,6},{8,9},{9,8},{10,11... | collective-permute-start | bytes 393224 | tf_op jit(solution)/shard_map/ppermute | solution.py:284
  13.0 1.4 %collective-permute-start.9 = (f32[1,16,2048]{2,1,0:T(8,128)S(1)}, f32[1,16,2048]{2,1,0:T(8,128)S(1)}, u32[]{:S(2)}, u32[]{:S(2)}) collective-permute-start(f32[1,16,2048]{2,1,0:T(8,128)S(1)} %collective-permute-done.1.refs_2_.refs_4_), channel_id=1, source_target_pairs={{0,1},{1,0},{2,3},{3,2},{4,5},{5,4},{6,7},{7,6},{8,9},{9,8},{10,11... | collective-permute-start | bytes 393224 | tf_op jit(solution)/shard_map/ppermute | solution.py:284
  13.4 1.3 %collective-permute-start.10 = (f32[1,16,2048]{2,1,0:T(8,128)S(1)}, f32[1,16,2048]{2,1,0:T(8,128)S(1)}, u32[]{:S(2)}, u32[]{:S(2)}) collective-permute-start(f32[1,16,2048]{2,1,0:T(8,128)S(1)} %collective-permute-done.2.refs_3_.refs_5_), channel_id=1, source_target_pairs={{0,1},{1,0},{2,3},{3,2},{4,5},{5,4},{6,7},{7,6},{8,9},{9,8},{10,11... | collective-permute-start | bytes 393224 | tf_op jit(solution)/shard_map/ppermute | solution.py:284
